TPU v7x, 512 devices: a whole 4x4x16 slice. The times are simulated.
512 devices in a mesh: region: 64 (over y, z), sub: 8 (over x, core).
Axes of the slice: x: 4, y: 4, z: 16, core: 2. Of those that a mesh axis runs over, the one named last changes fastest.
Arguments:
- loads: bfloat16 [512, 32, 1024], P(('region', 'sub')), may hold values from -6 to 6
- index_blocks: int32 [512, 1024], P(('region', 'sub')), may hold values from 0 to 1023, each once within a row
- stiffness: bfloat16 [512, 1024, 1024], P(('region', 'sub')), as said below
- dirichlet: bfloat16 [512, 1024, 1024], P(('region', 'sub')), as said below
- modes: float32 [512, 6, 1024], P(('region', 'sub')), may hold values from -0.25 to 0.25
- coarse: float32 [3072, 3072], P(('region', 'sub')), as said below
Outputs:
- multiplier: float32 [512, 32, 1024], P(('region', 'sub'))
- projected: float32 [512, 32, 1024], P(('region', 'sub'))
Inputs may be any that keep to these rules, and one draw needn't show every extreme that they name: Each row of index_blocks holds every number 0 to 1023 once. `stiffness`: each subdomain's matrix is symmetric. `dirichlet`: each subdomain's matrix is symmetric. `coarse`: symmetric.
All inputs are finite; a program needn't handle non-finite values.
Results may differ from a plain program's by a relative error of at most 0.0068.
Values sent between devices are 32-bit elements; how exact they have to be, the bound alone decides.
A program may use at most 64 MiB of HBM per device.

v0:
```python
import jax
import jax.numpy as jnp
from jax import lax
from jax.sharding import PartitionSpec as P


def shifted(block, axis, distance):
    devices = range(lax.axis_size(axis))
    route = [((i - distance) % len(devices), i) for i in devices]
    return lax.ppermute(block, axis, route)


def on_device(loads, index_blocks, stiffness, dirichlet, modes, coarse):
    highest = lax.Precision.HIGHEST
    slot_map = index_blocks[0]
    stiff_matrix = stiffness[0]
    dirich_matrix = dirichlet[0]
    shapes = modes[0]
    forces = loads[0]
    cases = forces.shape[0]
    width = slot_map.shape[0]
    block = width // 8

    def apply_local(matrix, vector):
        local = jnp.zeros((cases, width), jnp.float32).at[:, slot_map].set(vector)
        product = jnp.dot(local.astype(jnp.bfloat16), matrix, preferred_element_type=jnp.float32)
        return jnp.take(product, slot_map, axis=1)

    def jump(field):
        from_next_sub = shifted(field[:, 2 * block : 4 * block], "sub", -1)
        from_prev_sub = shifted(field[:, 0 : 2 * block], "sub", 1)
        from_next_region = shifted(field[:, 6 * block : 8 * block], "region", -1)
        from_prev_region = shifted(field[:, 4 * block : 6 * block], "region", 1)
        partner = jnp.concatenate(
            [from_next_sub, from_prev_sub, from_next_region, from_prev_region], axis=1
        )
        return field - partner

    def local_terms(field):
        return jnp.einsum("kb,rb->kr", shapes, field, precision=highest)

    def gather_terms(field):
        return lax.all_gather(local_terms(field), ("region", "sub"), axis=0, tiled=True)

    def correction(terms):
        values = jnp.dot(coarse, terms, precision=highest)
        own_rigid = jnp.einsum("kr,kb->rb", values, shapes, precision=highest)
        return jump(own_rigid)

    def project(field):
        return field - correction(gather_terms(field))

    load_image = jnp.take(
        jnp.dot(forces, stiff_matrix, preferred_element_type=jnp.float32), slot_map, axis=1
    )
    residual = jump(load_image)
    terms = gather_terms(residual)
    projected = residual - correction(terms)
    search = project(jump(apply_local(dirich_matrix, projected)))
    rho = lax.psum(jnp.sum(residual * search, axis=1), ("region", "sub"))
    image = jump(apply_local(stiff_matrix, search))
    alpha = rho / lax.psum(jnp.sum(search * image, axis=1), ("region", "sub"))
    multiplier = alpha[:, None] * search
    residual = residual - alpha[:, None] * image
    projected = project(residual)
    return (multiplier[None], projected[None])


def solution(mesh):
    return jax.shard_map(
        on_device,
        mesh=mesh,
        in_specs=(
            P(("region", "sub"), None, None),
            P(("region", "sub"), None),
            P(("region", "sub"), None, None),
            P(("region", "sub"), None, None),
            P(("region", "sub"), None, None),
            P(("region", "sub"), None),
        ),
        out_specs=(P(("region", "sub"), None, None), P(("region", "sub"), None, None)),
        check_vma=False,
    )
```

profile of v0, /device:TPU:1, one launch (start us, length us, event | category | flops | bytes accessed | tf_op | source)
XLA Modules:
  0.0 591.3 jit_solution(2926533764517069616)
XLA Ops:
  0.6 0.8 compare_and_fusion
  1.5 0.7 fusion.33
  2.2 1.8 fusion.4
  4.0 2.8 gather_fusion
  6.8 0.2 copy.25
  7.1 6.9 %collective-permute-start = (f32[32,256]{1,0:T(8,128)S(1)}, f32[32,256]{1,0:T(8,128)S(1)}, u32[]{:S(2)}, u32[]{:S(2)}) collective-permute-start(f32[32,256]{1,0:T(8,128)S(1)} %get-tuple-element.27), channel_id=1, source_target_pairs={{1,0},{2,1},{3,2},{4,3},{5,4},{6,5},{7,6},{0,7},{9,8},{10,9},{11,1... | collective-permute-start | bytes 98312 | tf_op jit(solution)/shard_map/ppermute | solution.py:10
  13.9 1.9 collective-permute-start.3
  15.9 8.2 %collective-permute-start.2 = (f32[32,256]{1,0:T(8,128)S(1)}, f32[32,256]{1,0:T(8,128)S(1)}, u32[]{:S(2)}, u32[]{:S(2)}) collective-permute-start(f32[32,256]{1,0:T(8,128)S(1)} %get-tuple-element.29), channel_id=1, source_target_pairs={{8,0},{16,8},{24,16},{32,24},{40,32},{48,40},{56,48},{64,56},{72,6... | collective-permute-start | bytes 98312 | tf_op jit(solution)/shard_map/ppermute | solution.py:10
  24.1 1.4 collective-permute-start.1
  25.5 1.8 collective-permute-done.1
  27.3 0.2 convolution_bitcast_fusion.2
  27.5 123.1 %all-gather = f32[512,6,32]{2,1,0:T(8,128)} all-gather(f32[1,6,32]{2,1,0:T(8,128)S(1)} %convolution_bitcast_fusion.2), channel_id=1, replica_groups=mesh['region'=64,'sub'=8] {'region','sub'}, dimensions={0}, use_global_device_ids=true | all-gather | bytes 393984 | tf_op jit(solution)/shard_map/all_gather | solution.py:43
  150.6 2.6 reshape.82
  153.1 2.3 fusion.41
  155.5 0.4 fusion.24
  155.8 0.2 collective-permute-start.4
  156.0 1.9 collective-permute-start.7
  157.9 6.7 %collective-permute-start.6 = (f32[32,256]{1,0:T(8,128)S(1)}, f32[32,256]{1,0:T(8,128)S(1)}, u32[]{:S(2)}, u32[]{:S(2)}) collective-permute-start(f32[32,256]{1,0:T(8,128)S(1)} %get-tuple-element.25), channel_id=1, source_target_pairs={{8,0},{16,8},{24,16},{32,24},{40,32},{48,40},{56,48},{64,56},{72,6... | collective-permute-start | bytes 98312 | tf_op jit(solution)/shard_map/ppermute | solution.py:10
  164.6 2.2 collective-permute-start.5
  166.8 1.0 collective-permute-done.5
  167.8 0.2 copy.26
  168.0 3.2 scatter_custom_fusion
  171.3 2.5 fusion
  173.8 2.8 gather_fusion.1
  176.6 0.2 copy.28
  176.8 3.0 collective-permute-start.8
  179.8 1.9 collective-permute-start.11
  181.7 6.7 %collective-permute-start.10 = (f32[32,256]{1,0:T(8,128)S(1)}, f32[32,256]{1,0:T(8,128)S(1)}, u32[]{:S(2)}, u32[]{:S(2)}) collective-permute-start(f32[32,256]{1,0:T(8,128)S(1)} %get-tuple-element.21), channel_id=1, source_target_pairs={{8,0},{16,8},{24,16},{32,24},{40,32},{48,40},{56,48},{64,56},{72,6... | collective-permute-start | bytes 98312 | tf_op jit(solution)/shard_map/ppermute | solution.py:10
  188.4 1.0 collective-permute-done.10
  189.4 0.3 collective-permute-done.9
  189.7 0.2 convolution_bitcast_fusion.1
  189.9 123.3 %all-gather.1 = f32[512,6,32]{2,1,0:T(8,128)} all-gather(f32[1,6,32]{2,1,0:T(8,128)S(1)} %convolution_bitcast_fusion.1), channel_id=1, replica_groups=mesh['region'=64,'sub'=8] {'region','sub'}, dimensions={0}, use_global_device_ids=true | all-gather | bytes 393984 | tf_op jit(solution)/shard_map/all_gather | solution.py:43
  313.1 2.5 reshape.84
  315.7 2.3 fusion.42
  318.0 0.4 fusion.21
  318.4 0.2 collective-permute-start.12
  318.6 1.9 collective-permute-start.15
  320.5 6.7 %collective-permute-start.14 = (f32[32,256]{1,0:T(8,128)S(1)}, f32[32,256]{1,0:T(8,128)S(1)}, u32[]{:S(2)}, u32[]{:S(2)}) collective-permute-start(f32[32,256]{1,0:T(8,128)S(1)} %get-tuple-element.17), channel_id=1, source_target_pairs={{8,0},{16,8},{24,16},{32,24},{40,32},{48,40},{56,48},{64,56},{72,6... | collective-permute-start | bytes 98312 | tf_op jit(solution)/shard_map/ppermute | solution.py:10
  327.2 2.2 collective-permute-start.13
  329.3 1.0 collective-permute-done.13
  330.4 0.2 copy.29
  330.6 3.2 scatter_custom_fusion.1
  333.8 0.9 fusion.2
  334.7 2.8 gather_fusion.2
  337.5 0.2 copy.31
  337.8 2.8 collective-permute-start.16
  340.5 1.9 collective-permute-start.19
  342.4 6.7 %collective-permute-start.18 = (f32[32,256]{1,0:T(8,128)S(1)}, f32[32,256]{1,0:T(8,128)S(1)}, u32[]{:S(2)}, u32[]{:S(2)}) collective-permute-start(f32[32,256]{1,0:T(8,128)S(1)} %get-tuple-element.13), channel_id=1, source_target_pairs={{8,0},{16,8},{24,16},{32,24},{40,32},{48,40},{56,48},{64,56},{72,6... | collective-permute-start | bytes 98312 | tf_op jit(solution)/shard_map/ppermute | solution.py:10
  349.1 0.2 collective-permute-start.17
  349.3 0.8 collective-permute-done.18
  350.1 0.3 collective-permute-done.17
  350.4 0.1 multiply_reduce_fusion
  350.6 101.9 %all-reduce = (f32[32]{0:T(128)S(1)}, f32[32]{0:T(128)S(1)}) all-reduce(f32[32]{0:T(128)S(1)} %get-tuple-element.4, f32[32]{0:T(128)S(1)} %get-tuple-element.3), channel_id=1, replica_groups=mesh['region'=64,'sub'=8] {'region','sub'}, use_global_device_ids=true, to_apply=%region_2.4 | all-reduce | flops 64 | bytes 512 | tf_op jit(solution)/shard_map/psum | solution.py:60
  452.5 0.3 convolution_bitcast_fusion
  452.8 120.5 %all-gather.2 = f32[512,6,32]{2,1,0:T(8,128)} all-gather(f32[1,6,32]{2,1,0:T(8,128)S(1)} %convolution_bitcast_fusion), channel_id=1, replica_groups=mesh['region'=64,'sub'=8] {'region','sub'}, dimensions={0}, use_global_device_ids=true | all-gather | bytes 393984 | tf_op jit(solution)/shard_map/all_gather | solution.py:43
  573.3 2.5 reshape.86
  575.8 2.3 fusion.43
  578.1 0.4 fusion.18
  578.5 0.2 collective-permute-start.20
  578.7 2.2 collective-permute-start.23
  580.9 6.4 %collective-permute-start.22 = (f32[32,256]{1,0:T(8,128)S(1)}, f32[32,256]{1,0:T(8,128)S(1)}, u32[]{:S(2)}, u32[]{:S(2)}) collective-permute-start(f32[32,256]{1,0:T(8,128)S(1)} %get-tuple-element.9), channel_id=1, source_target_pairs={{8,0},{16,8},{24,16},{32,24},{40,32},{48,40},{56,48},{64,56},{72,6... | collective-permute-start | bytes 98312 | tf_op jit(solution)/shard_map/ppermute | solution.py:10
  587.3 2.2 collective-permute-start.21
  589.5 1.0 collective-permute-done.21
  590.5 0.8 fusion.16
  (39 shorter events, 0.3 us)
Async XLA Ops:
  0.6 1.6 copy-start
  2.2 25.0 %copy-start.1 = (f32[1,6,1024]{2,0,1:T(1,128)S(1)}, f32[1,6,1024]{2,0,1:T(1,128)}, u32[]{:S(2)}) copy-start(f32[1,6,1024]{2,0,1:T(1,128)} %param.12) | copy-start | bytes 73732
  7.1 18.4 %collective-permute-start = (f32[32,256]{1,0:T(8,128)S(1)}, f32[32,256]{1,0:T(8,128)S(1)}, u32[]{:S(2)}, u32[]{:S(2)}) collective-permute-start(f32[32,256]{1,0:T(8,128)S(1)} %get-tuple-element.27), channel_id=1, source_target_pairs={{1,0},{2,1},{3,2},{4,3},{5,4},{6,5},{7,6},{0,7},{9,8},{10,9},{11,1... | collective-permute-start | bytes 98312 | tf_op jit(solution)/shard_map/ppermute | solution.py:10
  13.9 11.5 %collective-permute-start.3 = (f32[32,256]{1,0:T(8,128)S(1)}, f32[32,256]{1,0:T(8,128)S(1)}, u32[]{:S(2)}, u32[]{:S(2)}) collective-permute-start(f32[32,256]{1,0:T(8,128)S(1)} %get-tuple-element.28), channel_id=1, source_target_pairs={{504,0},{0,8},{8,16},{16,24},{24,32},{32,40},{40,48},{48,56},{56,6... | collective-permute-start | bytes 98312 | tf_op jit(solution)/shard_map/ppermute | solution.py:10
  15.9 9.6 %collective-permute-start.2 = (f32[32,256]{1,0:T(8,128)S(1)}, f32[32,256]{1,0:T(8,128)S(1)}, u32[]{:S(2)}, u32[]{:S(2)}) collective-permute-start(f32[32,256]{1,0:T(8,128)S(1)} %get-tuple-element.29), channel_id=1, source_target_pairs={{8,0},{16,8},{24,16},{32,24},{40,32},{48,40},{56,48},{64,56},{72,6... | collective-permute-start | bytes 98312 | tf_op jit(solution)/shard_map/ppermute | solution.py:10
  24.1 3.2 collective-permute-start.1
  150.6 2.6 copy-start.2
  150.6 16.2 %copy-start.3 = (s32[1,1024]{1,0:T(1,128)S(1)}, s32[1,1024]{1,0:T(1,128)}, u32[]{:S(2)}) copy-start(s32[1,1024]{1,0:T(1,128)} %param.9) | copy-start | bytes 12292
  155.8 10.9 %collective-permute-start.4 = (f32[32,256]{1,0:T(8,128)S(1)}, f32[32,256]{1,0:T(8,128)S(1)}, u32[]{:S(2)}, u32[]{:S(2)}) collective-permute-start(f32[32,256]{1,0:T(8,128)S(1)} %get-tuple-element.23), channel_id=1, source_target_pairs={{1,0},{2,1},{3,2},{4,3},{5,4},{6,5},{7,6},{0,7},{9,8},{10,9},{11,1... | collective-permute-start | bytes 98312 | tf_op jit(solution)/shard_map/ppermute | solution.py:10
  156.0 10.8 %collective-permute-start.7 = (f32[32,256]{1,0:T(8,128)S(1)}, f32[32,256]{1,0:T(8,128)S(1)}, u32[]{:S(2)}, u32[]{:S(2)}) collective-permute-start(f32[32,256]{1,0:T(8,128)S(1)} %get-tuple-element.24), channel_id=1, source_target_pairs={{504,0},{0,8},{8,16},{16,24},{24,32},{32,40},{40,48},{48,56},{56,6... | collective-permute-start | bytes 98312 | tf_op jit(solution)/shard_map/ppermute | solution.py:10
  157.9 8.9 %collective-permute-start.6 = (f32[32,256]{1,0:T(8,128)S(1)}, f32[32,256]{1,0:T(8,128)S(1)}, u32[]{:S(2)}, u32[]{:S(2)}) collective-permute-start(f32[32,256]{1,0:T(8,128)S(1)} %get-tuple-element.25), channel_id=1, source_target_pairs={{8,0},{16,8},{24,16},{32,24},{40,32},{48,40},{56,48},{64,56},{72,6... | collective-permute-start | bytes 98312 | tf_op jit(solution)/shard_map/ppermute | solution.py:10
  164.6 3.2 collective-permute-start.5
  176.8 11.6 %collective-permute-start.8 = (f32[32,256]{1,0:T(8,128)S(1)}, f32[32,256]{1,0:T(8,128)S(1)}, u32[]{:S(2)}, u32[]{:S(2)}) collective-permute-start(f32[32,256]{1,0:T(8,128)S(1)} %get-tuple-element.19), channel_id=1, source_target_pairs={{1,0},{2,1},{3,2},{4,3},{5,4},{6,5},{7,6},{0,7},{9,8},{10,9},{11,1... | collective-permute-start | bytes 98312 | tf_op jit(solution)/shard_map/ppermute | solution.py:10
  179.8 8.6 %collective-permute-start.11 = (f32[32,256]{1,0:T(8,128)S(1)}, f32[32,256]{1,0:T(8,128)S(1)}, u32[]{:S(2)}, u32[]{:S(2)}) collective-permute-start(f32[32,256]{1,0:T(8,128)S(1)} %get-tuple-element.20), channel_id=1, source_target_pairs={{504,0},{0,8},{8,16},{16,24},{24,32},{32,40},{40,48},{48,56},{56,6... | collective-permute-start | bytes 98312 | tf_op jit(solution)/shard_map/ppermute | solution.py:10
  181.7 7.7 %collective-permute-start.10 = (f32[32,256]{1,0:T(8,128)S(1)}, f32[32,256]{1,0:T(8,128)S(1)}, u32[]{:S(2)}, u32[]{:S(2)}) collective-permute-start(f32[32,256]{1,0:T(8,128)S(1)} %get-tuple-element.21), channel_id=1, source_target_pairs={{8,0},{16,8},{24,16},{32,24},{40,32},{48,40},{56,48},{64,56},{72,6... | collective-permute-start | bytes 98312 | tf_op jit(solution)/shard_map/ppermute | solution.py:10
  188.4 1.3 collective-permute-start.9
  318.4 10.9 %collective-permute-start.12 = (f32[32,256]{1,0:T(8,128)S(1)}, f32[32,256]{1,0:T(8,128)S(1)}, u32[]{:S(2)}, u32[]{:S(2)}) collective-permute-start(f32[32,256]{1,0:T(8,128)S(1)} %get-tuple-element.15), channel_id=1, source_target_pairs={{1,0},{2,1},{3,2},{4,3},{5,4},{6,5},{7,6},{0,7},{9,8},{10,9},{11,1... | collective-permute-start | bytes 98312 | tf_op jit(solution)/shard_map/ppermute | solution.py:10
  318.6 10.8 %collective-permute-start.15 = (f32[32,256]{1,0:T(8,128)S(1)}, f32[32,256]{1,0:T(8,128)S(1)}, u32[]{:S(2)}, u32[]{:S(2)}) collective-permute-start(f32[32,256]{1,0:T(8,128)S(1)} %get-tuple-element.16), channel_id=1, source_target_pairs={{504,0},{0,8},{8,16},{16,24},{24,32},{32,40},{40,48},{48,56},{56,6... | collective-permute-start | bytes 98312 | tf_op jit(solution)/shard_map/ppermute | solution.py:10
  320.5 8.9 %collective-permute-start.14 = (f32[32,256]{1,0:T(8,128)S(1)}, f32[32,256]{1,0:T(8,128)S(1)}, u32[]{:S(2)}, u32[]{:S(2)}) collective-permute-start(f32[32,256]{1,0:T(8,128)S(1)} %get-tuple-element.17), channel_id=1, source_target_pairs={{8,0},{16,8},{24,16},{32,24},{40,32},{48,40},{56,48},{64,56},{72,6... | collective-permute-start | bytes 98312 | tf_op jit(solution)/shard_map/ppermute | solution.py:10
  327.2 3.2 collective-permute-start.13
  337.8 11.5 %collective-permute-start.16 = (f32[32,256]{1,0:T(8,128)S(1)}, f32[32,256]{1,0:T(8,128)S(1)}, u32[]{:S(2)}, u32[]{:S(2)}) collective-permute-start(f32[32,256]{1,0:T(8,128)S(1)} %get-tuple-element.11), channel_id=1, source_target_pairs={{1,0},{2,1},{3,2},{4,3},{5,4},{6,5},{7,6},{0,7},{9,8},{10,9},{11,1... | collective-permute-start | bytes 98312 | tf_op jit(solution)/shard_map/ppermute | solution.py:10
  340.5 8.8 %collective-permute-start.19 = (f32[32,256]{1,0:T(8,128)S(1)}, f32[32,256]{1,0:T(8,128)S(1)}, u32[]{:S(2)}, u32[]{:S(2)}) collective-permute-start(f32[32,256]{1,0:T(8,128)S(1)} %get-tuple-element.12), channel_id=1, source_target_pairs={{504,0},{0,8},{8,16},{16,24},{24,32},{32,40},{40,48},{48,56},{56,6... | collective-permute-start | bytes 98312 | tf_op jit(solution)/shard_map/ppermute | solution.py:10
  342.4 7.7 %collective-permute-start.18 = (f32[32,256]{1,0:T(8,128)S(1)}, f32[32,256]{1,0:T(8,128)S(1)}, u32[]{:S(2)}, u32[]{:S(2)}) collective-permute-start(f32[32,256]{1,0:T(8,128)S(1)} %get-tuple-element.13), channel_id=1, source_target_pairs={{8,0},{16,8},{24,16},{32,24},{40,32},{48,40},{56,48},{64,56},{72,6... | collective-permute-start | bytes 98312 | tf_op jit(solution)/shard_map/ppermute | solution.py:10
  349.1 1.3 collective-permute-start.17
  578.5 10.9 %collective-permute-start.20 = (f32[32,256]{1,0:T(8,128)S(1)}, f32[32,256]{1,0:T(8,128)S(1)}, u32[]{:S(2)}, u32[]{:S(2)}) collective-permute-start(f32[32,256]{1,0:T(8,128)S(1)} %get-tuple-element.7), channel_id=1, source_target_pairs={{1,0},{2,1},{3,2},{4,3},{5,4},{6,5},{7,6},{0,7},{9,8},{10,9},{11,1... | collective-permute-start | bytes 98312 | tf_op jit(solution)/shard_map/ppermute | solution.py:10
  578.7 10.8 %collective-permute-start.23 = (f32[32,256]{1,0:T(8,128)S(1)}, f32[32,256]{1,0:T(8,128)S(1)}, u32[]{:S(2)}, u32[]{:S(2)}) collective-permute-start(f32[32,256]{1,0:T(8,128)S(1)} %get-tuple-element.8), channel_id=1, source_target_pairs={{504,0},{0,8},{8,16},{16,24},{24,32},{32,40},{40,48},{48,56},{56,6... | collective-permute-start | bytes 98312 | tf_op jit(solution)/shard_map/ppermute | solution.py:10
  580.9 8.5 %collective-permute-start.22 = (f32[32,256]{1,0:T(8,128)S(1)}, f32[32,256]{1,0:T(8,128)S(1)}, u32[]{:S(2)}, u32[]{:S(2)}) collective-permute-start(f32[32,256]{1,0:T(8,128)S(1)} %get-tuple-element.9), channel_id=1, source_target_pairs={{8,0},{16,8},{24,16},{32,24},{40,32},{48,40},{56,48},{64,56},{72,6... | collective-permute-start | bytes 98312 | tf_op jit(solution)/shard_map/ppermute | solution.py:10
  587.3 3.2 collective-permute-start.21
where the time goes:
time: 592 us; the launch traced here: 591 us
  blocking collectives  469 us (79%)
  starting transfers between devices  74.3 us (13%)
  local copies, waits for them, and re-layouts  23.6 us (4%)
  matrix products  13.9 us (2%)
  waiting for transfers between devices  7.19 us (1%)
    all_gather x3, blocking collectives, gather_terms(): lax.all_gather(local_terms(field), ('region', 'sub'), axis=0, tiled=True)  367 us
    psum x1, blocking collectives, on_device(): rho = lax.psum(jnp.sum(residual * search, axis=1), ('region', 'sub'))  102 us
    ppermute x24, starting transfers between devices, shifted(): return lax.ppermute(block, axis, route)  74.3 us
  transfers between devices with their start and end apart: 24, of which 8 were waited for; matrix products, arithmetic and copies ran while one was open for 0% of the time, Pallas kernels for 0%

commit v1 on v0

v1 whole, which is shorter than its diff:
```python
import functools

import jax
import jax.numpy as jnp
import numpy as np
from jax import lax
from jax.experimental import pallas as pl
from jax.experimental.pallas import tpu as pltpu
from jax.sharding import PartitionSpec as P

MESH = pl.DeviceIdType.MESH
HIGHEST = lax.Precision.HIGHEST
F32 = jnp.float32
BF16 = jnp.bfloat16

WIDTH = 1024
CASES = 32
MODES = 6
QUARTER = WIDTH // 4
CHIPS_Z = 16
LANES = 128
GROUPS = LANES // CASES
NT = (((1,), (1,)), ((), ()))


def column_choice(nz, nu):
    choice = np.zeros((nz * nu * MODES, nu * LANES), np.float32)
    for z in range(nz):
        for u in range(nu):
            for i in range(MODES):
                lane = (i % GROUPS) * 32 + (i // GROUPS) * 16 + z
                choice[(z * nu + u) * MODES + i, u * LANES + lane] = 1.0
    return choice


def split3(x):
    hi = x.astype(BF16)
    rest = x - hi.astype(F32)
    mid = rest.astype(BF16)
    lo = (rest - mid.astype(F32)).astype(BF16)
    return jnp.concatenate([hi, mid, lo], axis=0)


def merge3(x):
    rows = x.shape[0] // 3
    return (x[:rows] + x[rows : 2 * rows]) + x[2 * rows :]


def kernel(
    ny, nz, nu,
    loads_in, index_in, stiff_in, dirich_in, modes_in, coarse_in, choice_in,
    mult_out, proj_out,
    loads_v, index_v, stiff_v, dirich_v, modes_v, coarse_v, choice_v,
    pick, pick_t, stiff_s, dirich_s,
    field, partner, shapes, other_shapes, weights,
    coarse_send, coarse_recv, xbuf, vsend, vrecv, nbuf,
    resid, projd, srch,
    in_sem, fsend, frecv, csend, crecv, gsend, grecv, psend, precv, nsend, nrecv,
):
    plane = ny * nu
    r = lax.axis_index("region")
    u = lax.axis_index("sub")
    y = lax.div(r, nz)
    z = lax.rem(r, nz)
    p = y * nu + u
    nr = ny * nz
    ahead_u, back_u = (r, lax.rem(u + 1, nu)), (r, lax.rem(u + nu - 1, nu))
    ahead_r, back_r = (lax.rem(r + 1, nr), u), (lax.rem(r + nr - 1, nr), u)

    def along_z(k):
        return (y * nz + lax.rem(z + k, nz), u)

    def in_plane(q):
        return (lax.div(q, nu) * nz + z, lax.rem(q, nu))

    loading = [
        pltpu.make_async_copy(a, b, in_sem.at[i])
        for i, (a, b) in enumerate(
            [
                (index_in, index_v),
                (loads_in, loads_v),
                (stiff_in, stiff_v),
                (modes_in, modes_v),
                (coarse_in, coarse_v),
                (choice_in, choice_v),
                (dirich_in, dirich_v),
            ]
        )
    ]
    for copy in loading:
        copy.start()

    barrier = pltpu.get_barrier_semaphore()

    def greet_z(k, _):
        pl.semaphore_signal(barrier, inc=1, device_id=along_z(k), device_id_type=MESH)
        return 0

    def greet_plane(k, _):
        pl.semaphore_signal(
            barrier, inc=1, device_id=in_plane(lax.rem(p + k, plane)), device_id_type=MESH
        )
        return 0

    lax.fori_loop(1, nz, greet_z, 0)
    lax.fori_loop(1, plane, greet_plane, 0)
    for there in (ahead_r, back_r):
        pl.semaphore_signal(barrier, inc=1, device_id=there, device_id_type=MESH)

    loading[0].wait()

    def build_pick(b, _):
        rows = pl.ds(pl.multiple_of(b * LANES, LANES), LANES)
        unknown = lax.broadcasted_iota(jnp.int32, (LANES, WIDTH), 0) + b * LANES
        pick[rows, :] = jnp.where(unknown == index_v[...], 1.0, 0.0).astype(BF16)
        return 0

    lax.fori_loop(0, WIDTH // LANES, build_pick, 0)

    loading[1].wait()
    loading[2].wait()
    product = jnp.dot(loads_v[...], stiff_v[...], preferred_element_type=F32)
    field[0] = merge3(jnp.dot(split3(product), pick[...], preferred_element_type=F32))

    loading[3].wait()
    shapes[...] = jnp.concatenate([modes_v[...], jnp.zeros((8 - MODES, WIDTH), F32)], axis=0)

    if nz < CHIPS_Z:
        xbuf[...] = jnp.zeros_like(xbuf)
    nbuf[...] = jnp.zeros_like(nbuf)

    pl.semaphore_wait(barrier, (nz - 1) + (plane - 1) + 2)

    def exchange(src, dst, at):
        routes = ((1, 0, back_u), (0, 1, ahead_u), (3, 2, back_r), (2, 3, ahead_r))
        copies = []
        for n, (have, want, there) in enumerate(routes):
            copies.append(
                pltpu.make_async_remote_copy(
                    src_ref=src.at[:, pl.ds(have * QUARTER, QUARTER)],
                    dst_ref=dst.at[:, pl.ds(want * QUARTER, QUARTER)],
                    send_sem=fsend.at[at, n],
                    recv_sem=frecv.at[at, n],
                    device_id=there,
                    device_id_type=MESH,
                )
            )
        for n in (2, 3, 0, 1):
            copies[n].start()
        return copies

    field_copies = [exchange(field.at[0], partner.at[0], 0)]
    shape_copies = exchange(shapes, other_shapes, 3)

    loading[4].wait()
    loading[5].wait()
    span = nz * nu * MODES
    own_rows = jnp.concatenate(
        [
            jnp.concatenate(
                [coarse_v[:, i * span : (i + 1) * span], jnp.zeros((8 - MODES, span), F32)], axis=0
            )
            for i in range(ny)
        ],
        axis=0,
    )
    sorted_rows = merge3(jnp.dot(split3(own_rows), choice_v[...], preferred_element_type=F32))
    row8 = lax.broadcasted_iota(jnp.int32, (8, LANES), 0)
    lane8 = lax.broadcasted_iota(jnp.int32, (8, LANES), 1)
    half8 = lax.rem(lax.div(lane8, 16), 2)
    group8 = lax.div(lane8, CASES)
    sums8 = jnp.where((row8 >= MODES) & (half8 == 1) & (group8 + GROUPS == row8), 1.0, 0.0)
    for q in range(plane):
        i, j = q // nu, q % nu
        coarse_send[q] = sorted_rows[8 * i : 8 * i + 8, LANES * j : LANES * (j + 1)] + sums8

    def send_coarse(k, _):
        q = lax.rem(p + k, plane)
        pltpu.make_async_remote_copy(
            src_ref=coarse_send.at[q],
            dst_ref=coarse_recv.at[p],
            send_sem=csend,
            recv_sem=crecv,
            device_id=in_plane(q),
            device_id_type=MESH,
        ).start()
        return 0

    lax.fori_loop(1, plane, send_coarse, 0)
    coarse_recv[pl.ds(p, 1)] = coarse_send[pl.ds(p, 1)]

    def wait_bytes(ref, sem):
        pltpu.make_async_copy(ref, ref, sem).wait()

    def build_pick_t(b, _):
        rows = pl.ds(pl.multiple_of(b * LANES, LANES), LANES)
        chunk = index_v[:, rows].astype(F32)
        column = jnp.broadcast_to(chunk, (LANES, LANES)).T
        unknown = lax.broadcasted_iota(jnp.int32, (LANES, WIDTH), 1).astype(F32)
        same = jnp.concatenate([column] * (WIDTH // LANES), axis=1) == unknown
        pick_t[rows, :] = jnp.where(same, 1.0, 0.0).astype(BF16)
        return 0

    lax.fori_loop(0, WIDTH // LANES, build_pick_t, 0)
    loading[6].wait()

    def to_slots(matrix, out, part):
        rows = pl.ds(part * QUARTER, QUARTER)
        half = jnp.dot(pick_t[rows, :], matrix[...], preferred_element_type=F32).astype(BF16)
        out[rows, :] = jnp.dot(half, pick[...], preferred_element_type=F32).astype(BF16)

    mine8 = lax.rem(row8, GROUPS) == group8

    def build_weights():
        for copy in shape_copies:
            copy.wait_recv()
        row = lax.broadcasted_iota(jnp.int32, (8, WIDTH), 0)
        block = lax.div(lax.broadcasted_iota(jnp.int32, (8, WIDTH), 1), QUARTER)
        for j in range(GROUPS):
            for h in range(2):
                at = (2 * j + h) * 8
                i = GROUPS * h + j
                if i < MODES:
                    weights[at : at + 8, :] = jnp.where(
                        row == 0,
                        shapes[i : i + 1, :],
                        jnp.where(row == block + 1, -other_shapes[i : i + 1, :], 0.0),
                    )
                else:
                    weights[at : at + 8, :] = jnp.zeros((8, WIDTH), F32)

    def coarse_terms(a, sums):
        terms = lax.dot_general(
            shapes[...], jnp.concatenate([a] * GROUPS, axis=0), NT,
            precision=HIGHEST, preferred_element_type=F32,
        )
        if sums is not None:
            row = lax.broadcasted_iota(jnp.int32, (8, 2 * LANES), 0)
            which = lax.div(lax.broadcasted_iota(jnp.int32, (8, 2 * LANES), 1), LANES)
            ones = jnp.where(row == which + MODES, 1.0, 0.0)
            narrow = jnp.concatenate(
                [sum(s[:, LANES * i : LANES * (i + 1)] for i in range(WIDTH // LANES)) for s in sums],
                axis=1,
            )
            terms = terms + lax.dot_general(
                ones, jnp.concatenate([narrow] * GROUPS, axis=0), NT,
                precision=HIGHEST, preferred_element_type=F32,
            )
        return jnp.where(mine8, terms, 0.0)

    def correction(at, a, sums, work):
        terms = coarse_terms(a, sums)
        for h in range(2):
            packed = jnp.sum(
                jnp.where(lax.div(row8, GROUPS) == h, terms, 0.0), axis=0, keepdims=True
            )
            xbuf[at, pl.ds(z, 1), h : h + 1, :] = packed[None]

        def send_terms(k, _):
            pltpu.make_async_remote_copy(
                src_ref=xbuf.at[at, z],
                dst_ref=xbuf.at[at, z],
                send_sem=gsend.at[at],
                recv_sem=grecv.at[at],
                device_id=along_z(k),
                device_id_type=MESH,
            ).start()
            return 0

        lax.fori_loop(1, nz, send_terms, 0)
        work[0]()
        if at == 0:
            wait_bytes(coarse_recv.at[pl.ds(0, plane - 1)], crecv)
        wait_bytes(xbuf.at[at, pl.ds(0, nz - 1)], grecv.at[at])
        line = jnp.concatenate([xbuf[at, :, 0, :], xbuf[at, :, 1, :]], axis=0)
        group = lax.div(lax.broadcasted_iota(jnp.int32, (2 * CHIPS_Z, LANES), 1), CASES)
        spread = []
        for j in range(GROUPS):
            own = jnp.where(group == j, line, 0.0)
            own = own + pltpu.roll(own, CASES, 1)
            spread.append(own + pltpu.roll(own, 2 * CASES, 1))
        part = jnp.dot(
            coarse_recv[...].reshape(plane * 8, LANES), jnp.concatenate(spread, axis=0),
            precision=HIGHEST, preferred_element_type=F32,
        ).reshape(plane, 8, LANES)
        part = jnp.where(mine8[None], part, 0.0)
        for h in range(2):
            vsend[at, :, h : h + 1, :] = jnp.sum(
                part[:, GROUPS * h : GROUPS * (h + 1), :], axis=1, keepdims=True
            )

        def send_part(k, _):
            q = lax.rem(p + k, plane)
            pltpu.make_async_remote_copy(
                src_ref=vsend.at[at, q],
                dst_ref=vrecv.at[at, p],
                send_sem=psend.at[at],
                recv_sem=precv.at[at],
                device_id=in_plane(q),
                device_id_type=MESH,
            ).start()
            return 0

        lax.fori_loop(1, plane, send_part, 0)
        vrecv[at, pl.ds(p, 1)] = vsend[at, pl.ds(p, 1)]
        work[1]()
        wait_bytes(vrecv.at[at, pl.ds(0, plane - 1)], precv.at[at])
        nbuf[at, 0] = jnp.sum(vrecv[at], axis=0)
        copies = []
        for n, there in enumerate((back_u, ahead_u, back_r, ahead_r)):
            copies.append(
                pltpu.make_async_remote_copy(
                    src_ref=nbuf.at[at, 0],
                    dst_ref=nbuf.at[at, n + 1],
                    send_sem=nsend.at[at, n],
                    recv_sem=nrecv.at[at, n],
                    device_id=there,
                    device_id_type=MESH,
                )
            )
        for copy in copies:
            copy.start()
        work[2]()
        for copy in copies:
            copy.wait_recv()
        halves = [nbuf[at, :, h, :] for h in range(2)]
        values = jnp.concatenate(
            [
                halves[h] if j == 0 else pltpu.roll(halves[h], LANES - CASES * j, 1)
                for j in range(GROUPS)
                for h in range(2)
            ],
            axis=0,
        ).T[:CASES]
        out = jnp.dot(values, weights[...], precision=HIGHEST, preferred_element_type=F32)
        return out, values, copies

    def finish(at, work):
        work()
        for copy in field_copies[at]:
            copy.wait_recv()
        return field[at] - partner[at]

    resid[...] = finish(0, lambda: to_slots(dirich_v, dirich_s, 0))
    correct, _, near0 = correction(
        0,
        resid[...],
        None,
        (
            lambda: to_slots(dirich_v, dirich_s, 1),
            lambda: to_slots(dirich_v, dirich_s, 2),
            lambda: (to_slots(dirich_v, dirich_s, 3), build_weights()),
        ),
    )
    projd[...] = resid[...] - correct

    field[1] = jnp.dot(projd[...].astype(BF16), dirich_s[...], preferred_element_type=F32)
    field_copies.append(exchange(field.at[1], partner.at[1], 1))
    srch[...] = finish(1, lambda: to_slots(stiff_v, stiff_s, 0))
    correct, _, near1 = correction(
        1,
        srch[...],
        None,
        tuple(functools.partial(to_slots, stiff_v, stiff_s, n) for n in (1, 2, 3)),
    )
    srch[...] = srch[...] - correct

    field[2] = jnp.dot(srch[...].astype(BF16), stiff_s[...], preferred_element_type=F32)
    field_copies.append(exchange(field.at[2], partner.at[2], 2))
    image = finish(2, lambda: None)
    correct, values, near2 = correction(
        2, image, (resid[...] * srch[...], srch[...] * image), (lambda: None,) * 3
    )
    at_rho = (2 * 2 + 1) * 8
    at_bend = (2 * 3 + 1) * 8
    alpha = values[:, at_rho : at_rho + 1] / values[:, at_bend : at_bend + 1]
    mult_out[0] = alpha * srch[...]
    proj_out[0] = projd[...] - alpha * (image - correct)

    for copies in field_copies + [shape_copies, near0, near1, near2]:
        for copy in copies:
            copy.wait_send()
    wait_bytes(coarse_send.at[pl.ds(0, plane - 1)], csend)
    for at in range(3):
        wait_bytes(xbuf.at[at, pl.ds(0, nz - 1)], gsend.at[at])
        wait_bytes(vsend.at[at, pl.ds(0, plane - 1)], psend.at[at])


def on_device(ny, nz, nu, loads, index_blocks, stiffness, dirichlet, modes, coarse):
    plane = ny * nu
    span = nz * nu * MODES
    choice = jnp.asarray(column_choice(nz, nu), BF16)
    dma = pltpu.SemaphoreType.DMA
    out = jax.ShapeDtypeStruct((1, CASES, WIDTH), F32)
    return pl.pallas_call(
        functools.partial(kernel, ny, nz, nu),
        out_shape=(out, out),
        in_specs=[pl.BlockSpec(memory_space=pl.ANY)] * 7,
        out_specs=[pl.BlockSpec(memory_space=pltpu.VMEM)] * 2,
        scratch_shapes=[
            pltpu.VMEM((CASES, WIDTH), BF16),
            pltpu.VMEM((1, WIDTH), jnp.int32),
            pltpu.VMEM((WIDTH, WIDTH), BF16),
            pltpu.VMEM((WIDTH, WIDTH), BF16),
            pltpu.VMEM((MODES, WIDTH), F32),
            pltpu.VMEM((MODES, ny * span), F32),
            pltpu.VMEM((span, nu * LANES), BF16),
            pltpu.VMEM((WIDTH, WIDTH), BF16),
            pltpu.VMEM((WIDTH, WIDTH), BF16),
            pltpu.VMEM((WIDTH, WIDTH), BF16),
            pltpu.VMEM((WIDTH, WIDTH), BF16),
            pltpu.VMEM((3, CASES, WIDTH), F32),
            pltpu.VMEM((3, CASES, WIDTH), F32),
            pltpu.VMEM((8, WIDTH), F32),
            pltpu.VMEM((8, WIDTH), F32),
            pltpu.VMEM((64, WIDTH), F32),
            pltpu.VMEM((plane, 8, LANES), F32),
            pltpu.VMEM((plane, 8, LANES), F32),
            pltpu.VMEM((3, CHIPS_Z, 2, LANES), F32),
            pltpu.VMEM((3, plane, 2, LANES), F32),
            pltpu.VMEM((3, plane, 2, LANES), F32),
            pltpu.VMEM((3, 8, 2, LANES), F32),
            pltpu.VMEM((CASES, WIDTH), F32),
            pltpu.VMEM((CASES, WIDTH), F32),
            pltpu.VMEM((CASES, WIDTH), F32),
            dma((7,)),
            dma((4, 4)),
            dma((4, 4)),
            dma,
            dma,
            dma((3,)),
            dma((3,)),
            dma((3,)),
            dma((3,)),
            dma((3, 4)),
            dma((3, 4)),
        ],
        compiler_params=pltpu.CompilerParams(
            collective_id=0, has_side_effects=True, vmem_limit_bytes=60 * 1024 * 1024
        ),
    )(
        loads[0], index_blocks, stiffness[0], dirichlet[0], modes[0], coarse, choice
    )


def solution(mesh):
    regions, nu = mesh.shape["region"], mesh.shape["sub"]
    nz = min(CHIPS_Z, regions // 2)
    both = ("region", "sub")
    return jax.shard_map(
        functools.partial(on_device, regions // nz, nz, nu),
        mesh=mesh,
        in_specs=(
            P(both, None, None),
            P(both, None),
            P(both, None, None),
            P(both, None, None),
            P(both, None, None),
            P(both, None),
        ),
        out_specs=(P(both, None, None), P(both, None, None)),
        check_vma=False,
    )
```

time: 592 us -> 88 us (0.15)
  blocking collectives: 469 us -> 0 us
  Pallas kernels: 0 us -> 82.6 us
  starting transfers between devices: 74.3 us -> 0 us
  local copies, waits for them, and re-layouts: 23.6 us -> 4.5 us
  matrix products: 13.9 us -> 0 us
  waiting for transfers between devices: 7.19 us -> 0 us
    all_gather x3 -> x0, blocking collectives: 367 us -> none  [gather_terms(): lax.all_gather(local_terms(field), ('region', 'sub'), axis=0, tiled=True)]
    psum x1 -> x0, blocking collectives: 102 us -> none  [on_device(): rho = lax.psum(jnp.sum(residual * search, axis=1), ('region', 'sub'))]
    pallas_call x0 -> x1, Pallas kernels: none -> 82.6 us  [on_device(): pl.pallas_call(functools.partial(kernel, ny, nz, nu), out_shape=(out, out...]
    ppermute x24 -> x0, starting transfers between devices: 74.3 us -> none  [shifted(): return lax.ppermute(block, axis, route)]
    dot_general x12 -> x0, matrix products: 13.9 us -> none  [the longest x3 6.97 us: correction(): values = jnp.dot(coarse, terms, precision=highest)]
    gather x6 -> x0, local copies, waits for them, and re-layouts: 8.94 us -> none  [the longest x4 5.96 us: apply_local(): return jnp.take(product, slot_map, axis=1)]
    ppermute x24 -> x0, waiting for transfers between devices: 7.19 us -> none  [shifted(): return lax.ppermute(block, axis, route)]
    scatter x2 -> x0, local copies, waits for them, and re-layouts: 6.43 us -> none  [apply_local(): local = jnp.zeros((cases, width), jnp.float32).at[:, slot_map].set(vector)]
  transfers between devices with their start and end apart: 24 -> 0, of which waited for: 8 -> 0; matrix products, arithmetic and copies ran while one was open for 0% -> 0% of each run, Pallas kernels for 0% -> 0%
where the time goes in v1:
time: 88 us; the launch traced here: 87.8 us
  Pallas kernels  82.6 us (94%)
  local copies, waits for them, and re-layouts  4.5 us (5%)
    pallas_call x1, Pallas kernels, on_device(): pl.pallas_call(functools.partial(kernel, ny, nz, nu), out_shape=(out, out...  82.6 us
    unnamed x3, local copies, waits for them, and re-layouts  4.5 us

profile of v1, /device:TPU:1, one launch (start us, length us, event | category | flops | bytes accessed | tf_op | source)
XLA Modules:
  0.0 87.8 jit_solution(16222955049005439057)
XLA Ops:
  0.6 1.4 %copy.11 = f32[1,6,1024]{2,1,0:T(8,128)} copy(f32[1,6,1024]{2,0,1:T(1,128)} %param.11) | data formatting | bytes 49152
  2.0 82.6 %shard_map.86 = (f32[1,32,1024]{2,1,0:T(8,128)}, f32[1,32,1024]{2,1,0:T(8,128)}) custom-call(bf16[32,1024]{1,0:T(8,128)(2,1)} %bitcast.9, s32[1,1024]{1,0:T(1,128)} %index_in.1, bf16[1024,1024]{1,0:T(8,128)(2,1)} %bitcast.6, bf16[1024,1024]{1,0:T(8,128)(2,1)} %bitcast.7, f32[6,1024]{1,0:T(8,128)} %bitcast.8, f32[6,3072]{1,0:T(8,128)} %coarse_in.1, ...), custom_call_target="tpu_custom_call" | custom-call | tf_op jit(solution)/shard_map/pallas_call | solution.py:395
  84.6 1.6 %copy.14 = f32[1,32,1024]{2,1,0:T(8,128)} copy(f32[1,32,1024]{2,1,0:T(8,128)} %get-tuple-element.4) | data formatting | bytes 262144
  86.2 1.6 %copy.15 = f32[1,32,1024]{2,1,0:T(8,128)} copy(f32[1,32,1024]{2,1,0:T(8,128)} %get-tuple-element.5) | data formatting | bytes 262144

commit v2 on v1

v2 whole, which is shorter than its diff:
```python
import functools

import jax
import jax.numpy as jnp
from jax import lax
from jax.experimental import pallas as pl
from jax.experimental.pallas import tpu as pltpu
from jax.sharding import PartitionSpec as P

MESH = pl.DeviceIdType.MESH
HIGHEST = lax.Precision.HIGHEST
F32 = jnp.float32
BF16 = jnp.bfloat16

WIDTH = 1024
CASES = 32
MODES = 6
QUARTER = WIDTH // 4
CHIPS_Z = 16
LANES = 128
GROUPS = LANES // CASES
NT = (((1,), (1,)), ((), ()))


def split3(x):
    hi = x.astype(BF16)
    rest = x - hi.astype(F32)
    mid = rest.astype(BF16)
    lo = (rest - mid.astype(F32)).astype(BF16)
    return jnp.concatenate([hi, mid, lo], axis=0)


def merge3(x):
    rows = x.shape[0] // 3
    return (x[:rows] + x[rows : 2 * rows]) + x[2 * rows :]


def kernel(
    ny, nz, nu,
    loads_in, index_in, stiff_in, dirich_in, modes_in, coarse_in,
    mult_out, proj_out,
    loads_v, index_v, stiff_v, dirich_v, modes_v, coarse_v, choice,
    pick, pick_t, stiff_s, dirich_s,
    field, partner, shapes, other_shapes, to_ext, from_ext,
    coarse_send, coarse_recv, coarse_near, coarse_ext,
    xfirst, xbuf, vpart, vsend, vrecv, vrecv_r,
    resid, projd, srch,
    in_sem, fsend, frecv, csend, crecv, dsend, drecv, gsend, grecv, psend, precv, nsend, nrecv,
):
    plane = ny * nu
    r = lax.axis_index("region")
    u = lax.axis_index("sub")
    y = lax.div(r, nz)
    z = lax.rem(r, nz)
    p = y * nu + u
    nr = ny * nz
    ahead_u, back_u = (r, lax.rem(u + 1, nu)), (r, lax.rem(u + nu - 1, nu))
    ahead_r, back_r = (lax.rem(r + 1, nr), u), (lax.rem(r + nr - 1, nr), u)
    ahead_y, back_y = (lax.rem(r + nz, nr), u), (lax.rem(r + nr - nz, nr), u)

    def along_z(k):
        return (y * nz + lax.rem(z + k, nz), u)

    def in_plane(q, shift=0):
        return (lax.rem(lax.div(q, nu) * nz + z + (nr + shift), nr), lax.rem(q, nu))

    loading = [
        pltpu.make_async_copy(a, b, in_sem.at[i])
        for i, (a, b) in enumerate(
            [
                (index_in, index_v),
                (loads_in, loads_v),
                (stiff_in, stiff_v),
                (modes_in, modes_v),
                (coarse_in, coarse_v),
                (dirich_in, dirich_v),
            ]
        )
    ]
    for copy in loading:
        copy.start()

    barrier = pltpu.get_barrier_semaphore()

    def greet(there):
        pl.semaphore_signal(barrier, inc=1, device_id=there, device_id_type=MESH)

    def greet_z(k, _):
        greet(along_z(k))
        return 0

    def greet_plane(k, _):
        greet(in_plane(lax.rem(p + k, plane)))
        return 0

    def greet_near(k, _):
        q = lax.rem(p + k, plane)
        greet(in_plane(q, 1))
        greet(in_plane(q, -1))
        return 0

    lax.fori_loop(1, nz, greet_z, 0)
    lax.fori_loop(1, plane, greet_plane, 0)
    lax.fori_loop(0, plane, greet_near, 0)

    loading[0].wait()

    def build_pick(b, _):
        rows = pl.ds(pl.multiple_of(b * LANES, LANES), LANES)
        unknown = lax.broadcasted_iota(jnp.int32, (LANES, WIDTH), 0) + b * LANES
        pick[rows, :] = jnp.where(unknown == index_v[...], 1.0, 0.0).astype(BF16)
        return 0

    lax.fori_loop(0, WIDTH // LANES, build_pick, 0)

    loading[1].wait()
    loading[2].wait()
    product = jnp.dot(loads_v[...], stiff_v[...], preferred_element_type=F32)
    field[0] = merge3(jnp.dot(split3(product), pick[...], preferred_element_type=F32))

    loading[3].wait()
    shapes[...] = jnp.concatenate(
        [modes_v[:, 0, :], jnp.zeros((8 - MODES, WIDTH), F32)], axis=0
    )
    if nz < CHIPS_Z:
        xfirst[...] = jnp.zeros_like(xfirst)
        xbuf[...] = jnp.zeros_like(xbuf)

    pl.semaphore_wait(barrier, (nz - 1) + (plane - 1) + 2 * plane)

    def exchange(src, dst, at):
        routes = ((1, 0, back_u), (0, 1, ahead_u), (3, 2, back_r), (2, 3, ahead_r))
        copies = []
        for n, (have, want, there) in enumerate(routes):
            copies.append(
                pltpu.make_async_remote_copy(
                    src_ref=src.at[:, pl.ds(have * QUARTER, QUARTER)],
                    dst_ref=dst.at[:, pl.ds(want * QUARTER, QUARTER)],
                    send_sem=fsend.at[at, n],
                    recv_sem=frecv.at[at, n],
                    device_id=there,
                    device_id_type=MESH,
                )
            )
        for n in (2, 3, 0, 1):
            copies[n].start()
        return copies

    field_copies = [exchange(field.at[0], partner.at[0], 0)]
    shape_copies = exchange(shapes, other_shapes, 3)

    loading[4].wait()
    span = nz * nu * MODES
    place = lax.broadcasted_iota(jnp.int32, (1, nu * LANES), 1)
    mode = lax.rem(lax.div(place, 16), 2) * GROUPS + lax.rem(lax.div(place, 32), GROUPS)
    column = (lax.rem(place, 16) * nu + lax.div(place, LANES)) * MODES + mode
    column = jnp.where((mode < MODES) & (lax.rem(place, 16) < nz), column, -1)
    part = span // nz

    def build_choice(b, _):
        at = b * part
        if part % 16 == 0:
            at = pl.multiple_of(at, 16)
        row = lax.broadcasted_iota(jnp.int32, (part, nu * LANES), 0) + b * part
        choice[pl.ds(at, part), :] = jnp.where(row == column, 1.0, 0.0).astype(BF16)
        return 0

    lax.fori_loop(0, nz, build_choice, 0)
    own_rows = jnp.concatenate(
        [
            jnp.concatenate(
                [coarse_v[:, i * span : (i + 1) * span], jnp.zeros((8 - MODES, span), F32)], axis=0
            )
            for i in range(ny)
        ],
        axis=0,
    )
    sorted_rows = merge3(jnp.dot(split3(own_rows), choice[...], preferred_element_type=F32))
    row8 = lax.broadcasted_iota(jnp.int32, (8, LANES), 0)
    lane8 = lax.broadcasted_iota(jnp.int32, (8, LANES), 1)
    half8 = lax.rem(lax.div(lane8, 16), 2)
    group8 = lax.div(lane8, CASES)
    sums8 = jnp.where((row8 >= MODES) & (half8 == 1) & (group8 + GROUPS == row8), 1.0, 0.0)
    for q in range(plane):
        i, j = q // nu, q % nu
        coarse_send[q] = sorted_rows[8 * i : 8 * i + 8, LANES * j : LANES * (j + 1)] + sums8

    def send_coarse(k, _):
        q = lax.rem(p + k, plane)
        pltpu.make_async_remote_copy(
            src_ref=coarse_send.at[q],
            dst_ref=coarse_recv.at[p],
            send_sem=csend,
            recv_sem=crecv,
            device_id=in_plane(q),
            device_id_type=MESH,
        ).start()
        return 0

    lax.fori_loop(1, plane, send_coarse, 0)
    coarse_recv[pl.ds(p, 1)] = coarse_send[pl.ds(p, 1)]

    def wait_bytes(ref, sem):
        pltpu.make_async_copy(ref, ref, sem).wait()

    def build_pick_t(b, _):
        rows = pl.ds(pl.multiple_of(b * LANES, LANES), LANES)
        chunk = index_v[:, rows].astype(F32)
        column = jnp.broadcast_to(chunk, (LANES, LANES)).T
        unknown = lax.broadcasted_iota(jnp.int32, (LANES, WIDTH), 1).astype(F32)
        same = jnp.concatenate([column] * (WIDTH // LANES), axis=1) == unknown
        pick_t[rows, :] = jnp.where(same, 1.0, 0.0).astype(BF16)
        return 0

    lax.fori_loop(0, WIDTH // LANES, build_pick_t, 0)
    loading[5].wait()

    def to_slots(matrix, out, part):
        rows = pl.ds(part * QUARTER, QUARTER)
        half = jnp.dot(pick_t[rows, :], matrix[...], preferred_element_type=F32).astype(BF16)
        out[rows, :] = jnp.dot(half, pick[...], preferred_element_type=F32).astype(BF16)

    mine8 = lax.rem(row8, GROUPS) == group8
    vsend[...] = jnp.zeros_like(vsend)

    def build_weights():
        for copy in shape_copies:
            copy.wait_recv()
        block = lax.div(lax.broadcasted_iota(jnp.int32, (1, WIDTH), 1), QUARTER)
        nothing = jnp.zeros((1, WIDTH), F32)

        def mode_row(t, i):
            if t == 0:
                return shapes[i : i + 1, :]
            return jnp.where(block == t - 1, -other_shapes[i : i + 1, :], 0.0)

        rows_to = [nothing] * 32
        rows_from = [nothing] * 64
        for t in range(5):
            for i in range(MODES):
                h, j = divmod(i, GROUPS)
                row = mode_row(t, i)
                if t < 4:
                    rows_to[j * 8 + 2 * t + h] = row
                else:
                    rows_to[(2 + i % 2) * 8 + 2 * (i // 2) + 1] = row
                rows_from[j * 16 + (2 * t if t < 3 else 2 * t + 2) + h] = row
        for n in range(32):
            to_ext[n : n + 1, :] = rows_to[n]
        for n in range(64):
            from_ext[n : n + 1, :] = rows_from[n]

    def send_near_coarse():
        copies = []
        for n, there in enumerate((back_u, ahead_u, back_y, ahead_y)):
            copies.append(
                pltpu.make_async_remote_copy(
                    src_ref=coarse_recv,
                    dst_ref=coarse_near.at[n],
                    send_sem=dsend.at[n],
                    recv_sem=drecv.at[n],
                    device_id=there,
                    device_id_type=MESH,
                )
            )
        for copy in copies:
            copy.start()
        return copies

    def build_coarse_ext(copies):
        for copy in copies:
            copy.wait_recv()
        flat = (plane * 8, LANES)
        own = coarse_recv[...].reshape(flat)
        near = [coarse_near[n].reshape(flat) for n in range(4)]
        lane = lax.broadcasted_iota(jnp.int32, flat, 1)
        at_z = lax.rem(lane, 16)

        def roll(x, by):
            return pltpu.roll(x, by % LANES, 1) if by % LANES else x

        after = jnp.where(at_z == nz - 1, roll(near[2], nz - 1), roll(own, -1))
        before = jnp.where(at_z == 0, roll(near[3], 1 - nz), roll(own, 1))
        tiles = (own, near[0], near[1], after)
        for j in range(GROUPS):
            made = roll(tiles[0], -32 * j)
            for t in range(1, 4):
                made = jnp.where(lax.div(lane, 32) == t, roll(tiles[t], 32 * (t - j)), made)
            if j >= 2:
                for t in range(3):
                    h4, j4 = divmod(2 * t + j - 2, GROUPS)
                    moved = roll(before, 32 * t + 16 - 32 * j4 - 16 * h4)
                    made = jnp.where(lax.div(lane, 16) == 2 * t + 1, moved, made)
            coarse_ext[:, LANES * j : LANES * (j + 1)] = made

    def tiled(a):
        return jnp.concatenate([a] * GROUPS, axis=0)

    def spread(line):
        group = lax.div(lax.broadcasted_iota(jnp.int32, line.shape, 1), CASES)
        out = []
        for j in range(GROUPS):
            own = jnp.where(group == j, line, 0.0)
            own = own + pltpu.roll(own, CASES, 1)
            out.append(own + pltpu.roll(own, 2 * CASES, 1))
        return jnp.concatenate(out, axis=0)

    def send_line(at, ref):
        def send(k):
            pltpu.make_async_remote_copy(
                src_ref=ref.at[z],
                dst_ref=ref.at[z],
                send_sem=gsend.at[at],
                recv_sem=grecv.at[at],
                device_id=along_z(k),
                device_id_type=MESH,
            ).start()

        send(nz // 2)

        def both_ways(k, _):
            send(nz // 2 - k)
            send(nz // 2 + k)
            return 0

        lax.fori_loop(1, nz // 2, both_ways, 0)

    def first_terms(a):
        terms = lax.dot_general(
            shapes[...], tiled(a), NT, precision=HIGHEST, preferred_element_type=F32
        )
        terms = jnp.where(mine8, terms, 0.0)
        for h in range(2):
            packed = jnp.sum(
                jnp.where(lax.div(row8, GROUPS) == h, terms, 0.0), axis=0, keepdims=True
            )
            xfirst[pl.ds(z, 1), h : h + 1, :] = packed[None]
        send_line(0, xfirst)

    def first_product():
        wait_bytes(xfirst.at[pl.ds(0, nz - 1)], grecv.at[0])
        line = jnp.concatenate([xfirst[:, 0, :], xfirst[:, 1, :]], axis=0)
        return jnp.dot(
            coarse_recv[...].reshape(plane * 8, LANES), spread(line),
            precision=HIGHEST, preferred_element_type=F32,
        )

    def ext_terms(at, a, sums):
        terms = lax.dot_general(
            to_ext[...], tiled(a), NT, precision=HIGHEST, preferred_element_type=F32
        )
        if sums is not None:
            row = lax.broadcasted_iota(jnp.int32, (32, 2 * LANES), 0)
            which = lax.div(lax.broadcasted_iota(jnp.int32, (32, 2 * LANES), 1), LANES)
            ones = jnp.where(row == 8 * (which + 2) + 7, 1.0, 0.0)
            narrow = jnp.concatenate(
                [sum(s[:, LANES * i : LANES * (i + 1)] for i in range(WIDTH // LANES)) for s in sums],
                axis=1,
            )
            terms = terms + lax.dot_general(
                ones, tiled(narrow), NT, precision=HIGHEST, preferred_element_type=F32
            )
        packed = terms[:8]
        for j in range(1, GROUPS):
            packed = jnp.where(group8 == j, terms[8 * j : 8 * j + 8], packed)
        xbuf[at - 1, pl.ds(z, 1)] = packed[None]
        send_line(at, xbuf.at[at - 1])

    def ext_product(at):
        wait_bytes(xbuf.at[at - 1, pl.ds(0, nz - 1)], grecv.at[at])
        line = jnp.concatenate([xbuf[at - 1, :, n, :] for n in range(8)], axis=0)
        return jnp.dot(
            coarse_ext[...], spread(line), precision=HIGHEST, preferred_element_type=F32
        )

    def send_values(at, product):
        part = product.reshape(plane, 8, LANES)
        part = jnp.where(mine8[None], part, 0.0)
        for h in range(2):
            vpart[at, :, h : h + 1, :] = jnp.sum(
                part[:, GROUPS * h : GROUPS * (h + 1), :], axis=1, keepdims=True
            )

        def near(k, _):
            q = lax.rem(p + k, plane)
            for n, shift in enumerate((-1, 1)):
                pltpu.make_async_remote_copy(
                    src_ref=vpart.at[at, q],
                    dst_ref=vrecv_r.at[at, n, p],
                    send_sem=nsend.at[at, n],
                    recv_sem=nrecv.at[at, n],
                    device_id=in_plane(q, shift),
                    device_id_type=MESH,
                ).start()
            return 0

        lax.fori_loop(0, plane, near, 0)
        for i in range(ny):
            mine = vpart[at, nu * i : nu * (i + 1)]
            here = pl.ds(nu * i, nu)
            vsend[at, here, 0:2, :] = mine
            vsend[at, here, 2:4, :] = jnp.concatenate([mine[1:], mine[:1]], axis=0)
            vsend[at, here, 4:6, :] = jnp.concatenate([mine[nu - 1 :], mine[: nu - 1]], axis=0)

        def same(k, _):
            q = lax.rem(p + k, plane)
            pltpu.make_async_remote_copy(
                src_ref=vsend.at[at, q],
                dst_ref=vrecv.at[at, p],
                send_sem=psend.at[at],
                recv_sem=precv.at[at],
                device_id=in_plane(q),
                device_id_type=MESH,
            ).start()
            return 0

        lax.fori_loop(1, plane, same, 0)
        vrecv[at, pl.ds(p, 1)] = vsend[at, pl.ds(p, 1)]

    def rigid_jump(at):
        wait_bytes(vrecv.at[at, pl.ds(0, plane - 1)], precv.at[at])
        for n in range(2):
            wait_bytes(vrecv_r.at[at, n], nrecv.at[at, n])
        rows = jnp.concatenate(
            [jnp.sum(vrecv[at], axis=0)]
            + [jnp.sum(vrecv_r[at, n], axis=0) for n in range(2)]
            + [jnp.zeros((4, LANES), F32)],
            axis=0,
        )
        values = jnp.concatenate(
            [rows if j == 0 else pltpu.roll(rows, LANES - CASES * j, 1) for j in range(GROUPS)],
            axis=0,
        ).T[:CASES]
        out = jnp.dot(values, from_ext[...], precision=HIGHEST, preferred_element_type=F32)
        return out, values

    def jumped(at):
        for copy in field_copies[at]:
            copy.wait_recv()
        return field[at] - partner[at]

    to_slots(dirich_v, dirich_s, 0)
    resid[...] = jumped(0)
    first_terms(resid[...])
    to_slots(dirich_v, dirich_s, 1)
    to_slots(dirich_v, dirich_s, 2)
    wait_bytes(coarse_recv.at[pl.ds(0, plane - 1)], crecv)
    send_values(0, first_product())
    to_slots(dirich_v, dirich_s, 3)
    build_weights()
    correct, _ = rigid_jump(0)
    projd[...] = resid[...] - correct

    field[1] = jnp.dot(projd[...].astype(BF16), dirich_s[...], preferred_element_type=F32)
    ext_terms(1, field[1], None)
    field_copies.append(exchange(field.at[1], partner.at[1], 1))
    near_copies = send_near_coarse()
    to_slots(stiff_v, stiff_s, 0)
    to_slots(stiff_v, stiff_s, 1)
    build_coarse_ext(near_copies)
    send_values(1, ext_product(1))
    to_slots(stiff_v, stiff_s, 2)
    to_slots(stiff_v, stiff_s, 3)
    srch[...] = jumped(1)
    correct, _ = rigid_jump(1)
    srch[...] = srch[...] - correct

    field[2] = jnp.dot(srch[...].astype(BF16), stiff_s[...], preferred_element_type=F32)
    bend = field[2] * srch[...]
    ext_terms(2, field[2], (resid[...] * srch[...], bend + bend))
    field_copies.append(exchange(field.at[2], partner.at[2], 2))
    send_values(2, ext_product(2))
    image = jumped(2)
    correct, values = rigid_jump(2)
    alpha = values[:, 33:34] / values[:, 49:50]
    mult_out[0] = alpha * srch[...]
    proj_out[0] = projd[...] - alpha * (image - correct)

    for copies in field_copies + [shape_copies, near_copies]:
        for copy in copies:
            copy.wait_send()
    wait_bytes(coarse_send.at[pl.ds(0, plane - 1)], csend)
    wait_bytes(xfirst.at[pl.ds(0, nz - 1)], gsend.at[0])
    for at in range(3):
        if at:
            wait_bytes(xbuf.at[at - 1, pl.ds(0, nz - 1)], gsend.at[at])
        wait_bytes(vsend.at[at, pl.ds(0, plane - 1)], psend.at[at])
        for n in range(2):
            wait_bytes(vpart.at[at], nsend.at[at, n])


def on_device(ny, nz, nu, loads, index_blocks, stiffness, dirichlet, modes, coarse):
    plane = ny * nu
    span = nz * nu * MODES
    dma = pltpu.SemaphoreType.DMA
    out = jax.ShapeDtypeStruct((1, CASES, WIDTH), F32)
    return pl.pallas_call(
        functools.partial(kernel, ny, nz, nu),
        out_shape=(out, out),
        in_specs=[pl.BlockSpec(memory_space=pl.ANY)] * 6,
        out_specs=[pl.BlockSpec(memory_space=pltpu.VMEM)] * 2,
        scratch_shapes=[
            pltpu.VMEM((CASES, WIDTH), BF16),
            pltpu.VMEM((1, WIDTH), jnp.int32),
            pltpu.VMEM((WIDTH, WIDTH), BF16),
            pltpu.VMEM((WIDTH, WIDTH), BF16),
            pltpu.VMEM((MODES, 1, WIDTH), F32),
            pltpu.VMEM((MODES, ny * span), F32),
            pltpu.VMEM((span, nu * LANES), BF16),
            pltpu.VMEM((WIDTH, WIDTH), BF16),
            pltpu.VMEM((WIDTH, WIDTH), BF16),
            pltpu.VMEM((WIDTH, WIDTH), BF16),
            pltpu.VMEM((WIDTH, WIDTH), BF16),
            pltpu.VMEM((3, CASES, WIDTH), F32),
            pltpu.VMEM((3, CASES, WIDTH), F32),
            pltpu.VMEM((8, WIDTH), F32),
            pltpu.VMEM((8, WIDTH), F32),
            pltpu.VMEM((32, WIDTH), F32),
            pltpu.VMEM((64, WIDTH), F32),
            pltpu.VMEM((plane, 8, LANES), F32),
            pltpu.VMEM((plane, 8, LANES), F32),
            pltpu.VMEM((4, plane, 8, LANES), F32),
            pltpu.VMEM((plane * 8, GROUPS * LANES), F32),
            pltpu.VMEM((CHIPS_Z, 2, LANES), F32),
            pltpu.VMEM((2, CHIPS_Z, 8, LANES), F32),
            pltpu.VMEM((3, plane, 2, LANES), F32),
            pltpu.VMEM((3, plane, 8, LANES), F32),
            pltpu.VMEM((3, plane, 8, LANES), F32),
            pltpu.VMEM((3, 2, plane, 2, LANES), F32),
            pltpu.VMEM((CASES, WIDTH), F32),
            pltpu.VMEM((CASES, WIDTH), F32),
            pltpu.VMEM((CASES, WIDTH), F32),
            dma((6,)),
            dma((4, 4)),
            dma((4, 4)),
            dma,
            dma,
            dma((4,)),
            dma((4,)),
            dma((3,)),
            dma((3,)),
            dma((3,)),
            dma((3,)),
            dma((3, 2)),
            dma((3, 2)),
        ],
        compiler_params=pltpu.CompilerParams(
            collective_id=0, has_side_effects=True, vmem_limit_bytes=60 * 1024 * 1024
        ),
    )(
        loads[0],
        index_blocks,
        stiffness[0],
        dirichlet[0],
        jnp.transpose(modes, (1, 0, 2)),
        coarse,
    )


def solution(mesh):
    regions, nu = mesh.shape["region"], mesh.shape["sub"]
    nz = min(CHIPS_Z, regions // 2)
    both = ("region", "sub")
    return jax.shard_map(
        functools.partial(on_device, regions // nz, nz, nu),
        mesh=mesh,
        in_specs=(
            P(both, None, None),
            P(both, None),
            P(both, None, None),
            P(both, None, None),
            P(both, None, None),
            P(both, None),
        ),
        out_specs=(P(both, None, None), P(both, None, None)),
        check_vma=False,
    )
```

time: 88 us -> 74.5 us (0.85)
  Pallas kernels: 82.6 us -> 70.6 us
  local copies, waits for them, and re-layouts: 4.5 us -> 3.14 us
    pallas_call x1, Pallas kernels: 82.6 us -> 70.6 us  [on_device(): pl.pallas_call(functools.partial(kernel, ny, nz, nu), out_shape=(out, out...]
    unnamed x3 -> x2, local copies, waits for them, and re-layouts: 4.5 us -> 3.14 us
where the time goes in v2:
time: 74.5 us; the launch traced here: 74.3 us
  Pallas kernels  70.6 us (95%)
  local copies, waits for them, and re-layouts  3.14 us (4%)
    pallas_call x1, Pallas kernels, on_device(): pl.pallas_call(functools.partial(kernel, ny, nz, nu), out_shape=(out, out...  70.6 us
    unnamed x2, local copies, waits for them, and re-layouts  3.14 us

profile of v2, /device:TPU:1, one launch (start us, length us, event | category | flops | bytes accessed | tf_op | source)
XLA Modules:
  0.0 74.3 jit_solution(11003673423572045305)
XLA Ops:
  0.6 70.6 %shard_map.77 = (f32[1,32,1024]{2,1,0:T(8,128)}, f32[1,32,1024]{2,1,0:T(8,128)}) custom-call(bf16[32,1024]{1,0:T(8,128)(2,1)} %bitcast.6, s32[1,1024]{1,0:T(1,128)} %index_in.1, bf16[1024,1024]{1,0:T(8,128)(2,1)} %bitcast.4, bf16[1024,1024]{1,0:T(8,128)(2,1)} %bitcast.5, f32[6,1,1024]{2,1,0:T(1,128)} %bitcast.7, f32[6,3072]{1,0:T(8,128)} %coarse_in.1), custom_call_target="tpu_custom_call" | custom-call | tf_op jit(solution)/shard_map/pallas_call | solution.py:497
  71.2 1.6 %copy.10 = f32[1,32,1024]{2,1,0:T(8,128)} copy(f32[1,32,1024]{2,1,0:T(8,128)} %get-tuple-element.4) | data formatting | bytes 262144
  72.8 1.6 %copy.11 = f32[1,32,1024]{2,1,0:T(8,128)} copy(f32[1,32,1024]{2,1,0:T(8,128)} %get-tuple-element.5) | data formatting | bytes 262144

commit v3 on v2

--- a/solution.py
+++ b/solution.py
@@ -38,14 +38,14 @@
 def kernel(
     ny, nz, nu,
     loads_in, index_in, stiff_in, dirich_in, modes_in, coarse_in,
-    mult_out, proj_out,
+    srch_out, projd_out, step_out, alpha_out,
     loads_v, index_v, stiff_v, dirich_v, modes_v, coarse_v, choice,
     pick, pick_t, stiff_s, dirich_s,
-    field, partner, shapes, other_shapes, to_ext, from_ext,
+    field, partner, shapes, other_shapes, to_ext,
     coarse_send, coarse_recv, coarse_near, coarse_ext,
     xfirst, xbuf, vpart, vsend, vrecv, vrecv_r,
-    resid, projd, srch,
-    in_sem, fsend, frecv, csend, crecv, dsend, drecv, gsend, grecv, psend, precv, nsend, nrecv,
+    resid, projd, srch, moved, ratio, near_rows,
+    in_sem, out_sem, fsend, frecv, csend, crecv, dsend, drecv, gsend, grecv, psend, precv, nsend, nrecv,
 ):
     plane = ny * nu
     r = lax.axis_index("region")
@@ -61,9 +61,6 @@
     def along_z(k):
         return (y * nz + lax.rem(z + k, nz), u)
 
-    def in_plane(q, shift=0):
-        return (lax.rem(lax.div(q, nu) * nz + z + (nr + shift), nr), lax.rem(q, nu))
-
     loading = [
         pltpu.make_async_copy(a, b, in_sem.at[i])
         for i, (a, b) in enumerate(
@@ -85,23 +82,36 @@
     def greet(there):
         pl.semaphore_signal(barrier, inc=1, device_id=there, device_id_type=MESH)
 
+    def over_plane(visit):
+        subs = [lax.rem(u + k, nu) for k in range(nu)]
+
+        def row(k, _):
+            at_y = lax.rem(y + lax.rem(k + ny // 2 - 1, ny - 1) + 1, ny)
+            for at_u in subs:
+                visit(at_y, at_u, False)
+            return 0
+
+        lax.fori_loop(0, ny - 1, row, 0)
+        for k, at_u in enumerate(subs):
+            visit(y, at_u, k == 0)
+
+    def region_of(at_y, shift=0):
+        if shift == 0:
+            return at_y * nz + z
+        return lax.rem(at_y * nz + z + (nr + shift), nr)
+
     def greet_z(k, _):
         greet(along_z(k))
         return 0
 
-    def greet_plane(k, _):
-        greet(in_plane(lax.rem(p + k, plane)))
-        return 0
-
-    def greet_near(k, _):
-        q = lax.rem(p + k, plane)
-        greet(in_plane(q, 1))
-        greet(in_plane(q, -1))
-        return 0
+    def greet_plane(at_y, at_u, own):
+        greet((region_of(at_y, 1), at_u))
+        greet((region_of(at_y, -1), at_u))
+        if not own:
+            greet((region_of(at_y), at_u))
 
     lax.fori_loop(1, nz, greet_z, 0)
-    lax.fori_loop(1, plane, greet_plane, 0)
-    lax.fori_loop(0, plane, greet_near, 0)
+    over_plane(greet_plane)
 
     loading[0].wait()
 
@@ -185,19 +195,18 @@
         i, j = q // nu, q % nu
         coarse_send[q] = sorted_rows[8 * i : 8 * i + 8, LANES * j : LANES * (j + 1)] + sums8
 
-    def send_coarse(k, _):
-        q = lax.rem(p + k, plane)
-        pltpu.make_async_remote_copy(
-            src_ref=coarse_send.at[q],
-            dst_ref=coarse_recv.at[p],
-            send_sem=csend,
-            recv_sem=crecv,
-            device_id=in_plane(q),
-            device_id_type=MESH,
-        ).start()
-        return 0
-
-    lax.fori_loop(1, plane, send_coarse, 0)
+    def send_coarse(at_y, at_u, own):
+        if not own:
+            pltpu.make_async_remote_copy(
+                src_ref=coarse_send.at[at_y * nu + at_u],
+                dst_ref=coarse_recv.at[p],
+                send_sem=csend,
+                recv_sem=crecv,
+                device_id=(region_of(at_y), at_u),
+                device_id_type=MESH,
+            ).start()
+
+    over_plane(send_coarse)
     coarse_recv[pl.ds(p, 1)] = coarse_send[pl.ds(p, 1)]
 
     def wait_bytes(ref, sem):
@@ -235,7 +244,6 @@
             return jnp.where(block == t - 1, -other_shapes[i : i + 1, :], 0.0)
 
         rows_to = [nothing] * 32
-        rows_from = [nothing] * 64
         for t in range(5):
             for i in range(MODES):
                 h, j = divmod(i, GROUPS)
@@ -244,11 +252,8 @@
                     rows_to[j * 8 + 2 * t + h] = row
                 else:
                     rows_to[(2 + i % 2) * 8 + 2 * (i // 2) + 1] = row
-                rows_from[j * 16 + (2 * t if t < 3 else 2 * t + 2) + h] = row
         for n in range(32):
             to_ext[n : n + 1, :] = rows_to[n]
-        for n in range(64):
-            from_ext[n : n + 1, :] = rows_from[n]
 
     def send_near_coarse():
         copies = []
@@ -345,24 +350,26 @@
             precision=HIGHEST, preferred_element_type=F32,
         )
 
-    def ext_terms(at, a, sums):
-        terms = lax.dot_general(
-            to_ext[...], tiled(a), NT, precision=HIGHEST, preferred_element_type=F32
-        )
-        if sums is not None:
-            row = lax.broadcasted_iota(jnp.int32, (32, 2 * LANES), 0)
-            which = lax.div(lax.broadcasted_iota(jnp.int32, (32, 2 * LANES), 1), LANES)
-            ones = jnp.where(row == 8 * (which + 2) + 7, 1.0, 0.0)
-            narrow = jnp.concatenate(
-                [sum(s[:, LANES * i : LANES * (i + 1)] for i in range(WIDTH // LANES)) for s in sums],
-                axis=1,
-            )
-            terms = terms + lax.dot_general(
-                ones, tiled(narrow), NT, precision=HIGHEST, preferred_element_type=F32
-            )
+    def ext_of(rows, a):
+        return lax.dot_general(
+            rows, tiled(a), NT, precision=HIGHEST, preferred_element_type=F32
+        )
+
+    def inner(a, b):
+        both = a * b
+        narrow = sum(both[:, LANES * i : LANES * (i + 1)] for i in range(WIDTH // LANES))
+        return ext_of(jnp.ones((8, LANES), F32), narrow)[:1]
+
+    def exact(a, matrix):
+        return merge3(jnp.dot(split3(a), matrix[...], preferred_element_type=F32))
+
+    def send_ext(at, terms, sums):
         packed = terms[:8]
         for j in range(1, GROUPS):
             packed = jnp.where(group8 == j, terms[8 * j : 8 * j + 8], packed)
+        if sums is not None:
+            packed = jnp.where((row8 == 7) & (group8 == 2), sums[0], packed)
+            packed = jnp.where((row8 == 7) & (group8 == 3), sums[1], packed)
         xbuf[at - 1, pl.ds(z, 1)] = packed[None]
         send_line(at, xbuf.at[at - 1])
 
@@ -381,20 +388,18 @@
                 part[:, GROUPS * h : GROUPS * (h + 1), :], axis=1, keepdims=True
             )
 
-        def near(k, _):
-            q = lax.rem(p + k, plane)
+        def near(at_y, at_u, own):
             for n, shift in enumerate((-1, 1)):
                 pltpu.make_async_remote_copy(
-                    src_ref=vpart.at[at, q],
+                    src_ref=vpart.at[at, at_y * nu + at_u],
                     dst_ref=vrecv_r.at[at, n, p],
                     send_sem=nsend.at[at, n],
                     recv_sem=nrecv.at[at, n],
-                    device_id=in_plane(q, shift),
+                    device_id=(region_of(at_y, shift), at_u),
                     device_id_type=MESH,
                 ).start()
-            return 0
-
-        lax.fori_loop(0, plane, near, 0)
+
+        over_plane(near)
         for i in range(ny):
             mine = vpart[at, nu * i : nu * (i + 1)]
             here = pl.ds(nu * i, nu)
@@ -402,37 +407,55 @@
             vsend[at, here, 2:4, :] = jnp.concatenate([mine[1:], mine[:1]], axis=0)
             vsend[at, here, 4:6, :] = jnp.concatenate([mine[nu - 1 :], mine[: nu - 1]], axis=0)
 
-        def same(k, _):
-            q = lax.rem(p + k, plane)
-            pltpu.make_async_remote_copy(
-                src_ref=vsend.at[at, q],
-                dst_ref=vrecv.at[at, p],
-                send_sem=psend.at[at],
-                recv_sem=precv.at[at],
-                device_id=in_plane(q),
-                device_id_type=MESH,
-            ).start()
-            return 0
-
-        lax.fori_loop(1, plane, same, 0)
+        def same(at_y, at_u, own):
+            if not own:
+                pltpu.make_async_remote_copy(
+                    src_ref=vsend.at[at, at_y * nu + at_u],
+                    dst_ref=vrecv.at[at, p],
+                    send_sem=psend.at[at],
+                    recv_sem=precv.at[at],
+                    device_id=(region_of(at_y), at_u),
+                    device_id_type=MESH,
+                ).start()
+
+        over_plane(same)
         vrecv[at, pl.ds(p, 1)] = vsend[at, pl.ds(p, 1)]
 
-    def rigid_jump(at):
+    def values_here(at):
         wait_bytes(vrecv.at[at, pl.ds(0, plane - 1)], precv.at[at])
         for n in range(2):
             wait_bytes(vrecv_r.at[at, n], nrecv.at[at, n])
-        rows = jnp.concatenate(
-            [jnp.sum(vrecv[at], axis=0)]
-            + [jnp.sum(vrecv_r[at, n], axis=0) for n in range(2)]
-            + [jnp.zeros((4, LANES), F32)],
-            axis=0,
-        )
-        values = jnp.concatenate(
+        near_rows[0:8, :] = jnp.sum(vrecv[at], axis=0)
+        near_rows[6:8, :] = jnp.sum(vrecv_r[at, 0], axis=0)
+        near_rows[8:10, :] = jnp.sum(vrecv_r[at, 1], axis=0)
+        rows = near_rows[0:8, :]
+        sums = rows[1:2]
+        low, high = near_rows[8:9, :], near_rows[9:10, :]
+        spare = group8 >= 2
+        rows = jnp.where(spare & (row8 == 1), pltpu.roll(low, 2 * CASES, 1), rows)
+        rows = jnp.where(spare & (row8 == 3), low, rows)
+        rows = jnp.where(spare & (row8 == 5), pltpu.roll(high, 2 * CASES, 1), rows)
+        rows = jnp.where(spare & (row8 == 7), 0.0, rows)
+        return rows, sums
+
+    def by_case(rows):
+        return jnp.concatenate(
             [rows if j == 0 else pltpu.roll(rows, LANES - CASES * j, 1) for j in range(GROUPS)],
             axis=0,
-        ).T[:CASES]
-        out = jnp.dot(values, from_ext[...], precision=HIGHEST, preferred_element_type=F32)
-        return out, values
+        )
+
+    def rigid_jump(rows):
+        return jnp.dot(
+            by_case(rows).T[:CASES], to_ext[...], precision=HIGHEST, preferred_element_type=F32
+        )
+
+    def times(bend, rows):
+        return jnp.dot(bend, spread(rows), precision=HIGHEST, preferred_element_type=F32)
+
+    def bending(moved_rows):
+        return lax.dot_general(
+            moved_rows, to_ext[...], NT, precision=HIGHEST, preferred_element_type=F32
+        )
 
     def jumped(at):
         for copy in field_copies[at]:
@@ -442,39 +465,62 @@
     to_slots(dirich_v, dirich_s, 0)
     resid[...] = jumped(0)
     first_terms(resid[...])
-    to_slots(dirich_v, dirich_s, 1)
-    to_slots(dirich_v, dirich_s, 2)
+    for n in (1, 2, 3):
+        to_slots(dirich_v, dirich_s, n)
+    build_weights()
     wait_bytes(coarse_recv.at[pl.ds(0, plane - 1)], crecv)
     send_values(0, first_product())
-    to_slots(dirich_v, dirich_s, 3)
-    build_weights()
-    correct, _ = rigid_jump(0)
-    projd[...] = resid[...] - correct
-
+    moved[...] = exact(to_ext[...], dirich_s)
+    bend = bending(moved[...])
+    base = ext_of(moved[...], resid[...])
+    resid_terms = ext_of(to_ext[...], resid[...])
+    to_slots(stiff_v, stiff_s, 0)
+    to_slots(stiff_v, stiff_s, 1)
+    values, _ = values_here(0)
+
+    send_ext(1, base - times(bend, values), None)
+    projd[...] = resid[...] - rigid_jump(values)
     field[1] = jnp.dot(projd[...].astype(BF16), dirich_s[...], preferred_element_type=F32)
-    ext_terms(1, field[1], None)
     field_copies.append(exchange(field.at[1], partner.at[1], 1))
     near_copies = send_near_coarse()
-    to_slots(stiff_v, stiff_s, 0)
-    to_slots(stiff_v, stiff_s, 1)
+    to_slots(stiff_v, stiff_s, 2)
+    to_slots(stiff_v, stiff_s, 3)
     build_coarse_ext(near_copies)
     send_values(1, ext_product(1))
-    to_slots(stiff_v, stiff_s, 2)
-    to_slots(stiff_v, stiff_s, 3)
+    moved[...] = exact(to_ext[...], stiff_s)
+    bend = bending(moved[...])
     srch[...] = jumped(1)
-    correct, _ = rigid_jump(1)
-    srch[...] = srch[...] - correct
-
+    base = ext_of(moved[...], srch[...])
+    resid_inner = inner(resid[...], srch[...])
+    image_inner = inner(srch[...], exact(srch[...], stiff_s))
+    values, _ = values_here(1)
+
+    terms = base - times(bend, values)
+    each = spread(values)
+    rho = resid_inner - jnp.sum(each * resid_terms, axis=0, keepdims=True)
+    half = image_inner - jnp.sum(each * (base + terms), axis=0, keepdims=True)
+    send_ext(2, terms, (rho, half + half))
+    srch[...] = srch[...] - rigid_jump(values)
     field[2] = jnp.dot(srch[...].astype(BF16), stiff_s[...], preferred_element_type=F32)
-    bend = field[2] * srch[...]
-    ext_terms(2, field[2], (resid[...] * srch[...], bend + bend))
     field_copies.append(exchange(field.at[2], partner.at[2], 2))
+    done = [
+        pltpu.make_async_copy(a, b, out_sem.at[n])
+        for n, (a, b) in enumerate(
+            [(srch, srch_out), (projd, projd_out), (resid, step_out), (ratio, alpha_out)]
+        )
+    ]
+    done[0].start()
+    done[1].start()
     send_values(2, ext_product(2))
     image = jumped(2)
-    correct, values = rigid_jump(2)
-    alpha = values[:, 33:34] / values[:, 49:50]
-    mult_out[0] = alpha * srch[...]
-    proj_out[0] = projd[...] - alpha * (image - correct)
+    values, sums = values_here(2)
+    quotient = pltpu.roll(sums / pltpu.roll(sums, LANES - CASES, 1), 2 * CASES, 1)
+    ratio[...] = jnp.broadcast_to(quotient, (LANES, LANES)).T[:CASES]
+    done[3].start()
+    resid[...] = image - rigid_jump(values)
+    done[2].start()
+    for copy in done:
+        copy.wait()
 
     for copies in field_copies + [shape_copies, near_copies]:
         for copy in copies:
@@ -493,12 +539,12 @@
     plane = ny * nu
     span = nz * nu * MODES
     dma = pltpu.SemaphoreType.DMA
-    out = jax.ShapeDtypeStruct((1, CASES, WIDTH), F32)
-    return pl.pallas_call(
+    out = jax.ShapeDtypeStruct((CASES, WIDTH), F32)
+    search, projected, step, alpha = pl.pallas_call(
         functools.partial(kernel, ny, nz, nu),
-        out_shape=(out, out),
+        out_shape=(out, out, out, jax.ShapeDtypeStruct((CASES, LANES), F32)),
         in_specs=[pl.BlockSpec(memory_space=pl.ANY)] * 6,
-        out_specs=[pl.BlockSpec(memory_space=pltpu.VMEM)] * 2,
+        out_specs=[pl.BlockSpec(memory_space=pl.ANY)] * 4,
         scratch_shapes=[
             pltpu.VMEM((CASES, WIDTH), BF16),
             pltpu.VMEM((1, WIDTH), jnp.int32),
@@ -516,7 +562,6 @@
             pltpu.VMEM((8, WIDTH), F32),
             pltpu.VMEM((8, WIDTH), F32),
             pltpu.VMEM((32, WIDTH), F32),
-            pltpu.VMEM((64, WIDTH), F32),
             pltpu.VMEM((plane, 8, LANES), F32),
             pltpu.VMEM((plane, 8, LANES), F32),
             pltpu.VMEM((4, plane, 8, LANES), F32),
@@ -530,7 +575,11 @@
             pltpu.VMEM((CASES, WIDTH), F32),
             pltpu.VMEM((CASES, WIDTH), F32),
             pltpu.VMEM((CASES, WIDTH), F32),
+            pltpu.VMEM((32, WIDTH), F32),
+            pltpu.VMEM((CASES, LANES), F32),
+            pltpu.VMEM((16, LANES), F32),
             dma((6,)),
+            dma((4,)),
             dma((4, 4)),
             dma((4, 4)),
             dma,
@@ -555,6 +604,8 @@
         jnp.transpose(modes, (1, 0, 2)),
         coarse,
     )
+    alpha = alpha[:, :1]
+    return (alpha * search)[None], (projected - alpha * step)[None]
 
 
 def solution(mesh):

time: 74.5 us -> 70.7 us (0.949)
  Pallas kernels: 70.6 us -> 67.3 us
  local copies, waits for them, and re-layouts: 3.14 us -> 0.83 us
  other arithmetic: 0 us -> 1.82 us
    pallas_call x1, Pallas kernels: 70.6 us -> 67.3 us  [on_device(): pl.pallas_call(functools.partial(kernel, ny, nz, nu), out_shape=(out, out...]
    unnamed x2 -> x0, local copies, waits for them, and re-layouts: 3.14 us -> none
    broadcast_in_dim x0 -> x1, other arithmetic: none -> 1.82 us  [on_device(): return ((alpha * search)[None], (projected - alpha * step)[None])]
    slice x0 -> x1, local copies, waits for them, and re-layouts: none -> 0.83 us  [on_device(): alpha = alpha[:, :1]]
where the time goes in v3:
time: 70.7 us; the launch traced here: 70.6 us
  Pallas kernels  67.3 us (95%)
  other arithmetic  1.82 us (3%)
  local copies, waits for them, and re-layouts  0.83 us (1%)
    pallas_call x1, Pallas kernels, on_device(): pl.pallas_call(functools.partial(kernel, ny, nz, nu), out_shape=(out, out...  67.3 us
    broadcast_in_dim x1, other arithmetic, on_device(): return ((alpha * search)[None], (projected - alpha * step)[None])  1.82 us

profile of v3, /device:TPU:1, one launch (start us, length us, event | category | flops | bytes accessed | tf_op | source)
XLA Modules:
  0.0 70.6 jit_solution(12917821911200416065)
XLA Ops:
  0.6 67.3 %shard_map.77 = (f32[32,1024]{1,0:T(8,128)}, f32[32,1024]{1,0:T(8,128)}, f32[32,1024]{1,0:T(8,128)}, f32[32,128]{1,0:T(8,128)}) custom-call(bf16[32,1024]{1,0:T(8,128)(2,1)} %bitcast.10, s32[1,1024]{1,0:T(1,128)} %index_in.1, bf16[1024,1024]{1,0:T(8,128)(2,1)} %bitcast.8, bf16[1024,1024]{1,0:T(8,128)(2,1)} %bitcast.9, f32[6,1,1024]{2,1,0:T(1,128)} %bitcast.11, ...), custom_call_target="tpu_custom_call" | custom-call | tf_op jit(solution)/shard_map/pallas_call | solution.py:543
  67.9 0.8 %slice_reduce_fusion = f32[32]{0:T(128)S(1)} fusion(f32[32,128]{1,0:T(8,128)} %get-tuple-element.6), kind=kLoop, calls=%fused_computation.2 | loop fusion | bytes 256 | tf_op jit(solution)/shard_map/slice | solution.py:607
  68.7 1.8 %subtract_bitcast_fusion = (f32[1,32,1024]{2,1,0:T(8,128)}, f32[1,32,1024]{2,1,0:T(8,128)}) fusion(f32[32,1024]{1,0:T(8,128)} %get-tuple-element.8, f32[32,1024]{1,0:T(8,128)} %get-tuple-element.9, f32[32]{0:T(128)S(1)} %slice_reduce_fusion, f32[32,1024]{1,0:T(8,128)} %get-tuple-element.7), kind=kLoop, calls=%fused_computation | loop fusion | flops 98304 | bytes 655488 | tf_op jit(solution)/shard_map/broadcast_in_dim | solution.py:608

commit v4 on v3

--- a/solution.py
+++ b/solution.py
@@ -19,6 +19,7 @@
 CHIPS_Z = 16
 LANES = 128
 GROUPS = LANES // CASES
+NN = (((1,), (0,)), ((), ()))
 NT = (((1,), (1,)), ((), ()))
 
 
@@ -28,6 +29,18 @@
     mid = rest.astype(BF16)
     lo = (rest - mid.astype(F32)).astype(BF16)
     return jnp.concatenate([hi, mid, lo], axis=0)
+
+
+def product3(a, b, dims):
+    def split(x):
+        hi = x.astype(BF16)
+        return hi, (x - hi.astype(F32)).astype(BF16)
+
+    def dot(p, q):
+        return lax.dot_general(p, q, dims, preferred_element_type=F32)
+
+    (a_hi, a_lo), (b_hi, b_lo) = split(a), split(b)
+    return dot(a_hi, b_hi) + (dot(a_hi, b_lo) + dot(a_lo, b_hi))
 
 
 def merge3(x):
@@ -331,9 +344,7 @@
         lax.fori_loop(1, nz // 2, both_ways, 0)
 
     def first_terms(a):
-        terms = lax.dot_general(
-            shapes[...], tiled(a), NT, precision=HIGHEST, preferred_element_type=F32
-        )
+        terms = product3(shapes[...], tiled(a), NT)
         terms = jnp.where(mine8, terms, 0.0)
         for h in range(2):
             packed = jnp.sum(
@@ -345,10 +356,7 @@
     def first_product():
         wait_bytes(xfirst.at[pl.ds(0, nz - 1)], grecv.at[0])
         line = jnp.concatenate([xfirst[:, 0, :], xfirst[:, 1, :]], axis=0)
-        return jnp.dot(
-            coarse_recv[...].reshape(plane * 8, LANES), spread(line),
-            precision=HIGHEST, preferred_element_type=F32,
-        )
+        return product3(coarse_recv[...].reshape(plane * 8, LANES), spread(line), NN)
 
     def ext_of(rows, a):
         return lax.dot_general(
@@ -376,9 +384,7 @@
     def ext_product(at):
         wait_bytes(xbuf.at[at - 1, pl.ds(0, nz - 1)], grecv.at[at])
         line = jnp.concatenate([xbuf[at - 1, :, n, :] for n in range(8)], axis=0)
-        return jnp.dot(
-            coarse_ext[...], spread(line), precision=HIGHEST, preferred_element_type=F32
-        )
+        return product3(coarse_ext[...], spread(line), NN)
 
     def send_values(at, product):
         part = product.reshape(plane, 8, LANES)
@@ -445,12 +451,10 @@
         )
 
     def rigid_jump(rows):
-        return jnp.dot(
-            by_case(rows).T[:CASES], to_ext[...], precision=HIGHEST, preferred_element_type=F32
-        )
+        return product3(by_case(rows).T[:CASES], to_ext[...], NN)
 
     def times(bend, rows):
-        return jnp.dot(bend, spread(rows), precision=HIGHEST, preferred_element_type=F32)
+        return product3(bend, spread(rows), NN)
 
     def bending(moved_rows):
         return lax.dot_general(
@@ -515,7 +519,8 @@
     image = jumped(2)
     values, sums = values_here(2)
     quotient = pltpu.roll(sums / pltpu.roll(sums, LANES - CASES, 1), 2 * CASES, 1)
-    ratio[...] = jnp.broadcast_to(quotient, (LANES, LANES)).T[:CASES]
+    column = jnp.broadcast_to(quotient, (LANES, LANES)).T[:CASES]
+    ratio[...] = jnp.concatenate([column] * (WIDTH // LANES), axis=1)
     done[3].start()
     resid[...] = image - rigid_jump(values)
     done[2].start()
@@ -542,9 +547,9 @@
     out = jax.ShapeDtypeStruct((CASES, WIDTH), F32)
     search, projected, step, alpha = pl.pallas_call(
         functools.partial(kernel, ny, nz, nu),
-        out_shape=(out, out, out, jax.ShapeDtypeStruct((CASES, LANES), F32)),
+        out_shape=(pltpu.VMEM((CASES, WIDTH), F32),) * 4,
         in_specs=[pl.BlockSpec(memory_space=pl.ANY)] * 6,
-        out_specs=[pl.BlockSpec(memory_space=pl.ANY)] * 4,
+        out_specs=[pl.BlockSpec(memory_space=pltpu.VMEM)] * 4,
         scratch_shapes=[
             pltpu.VMEM((CASES, WIDTH), BF16),
             pltpu.VMEM((1, WIDTH), jnp.int32),
@@ -576,7 +581,7 @@
             pltpu.VMEM((CASES, WIDTH), F32),
             pltpu.VMEM((CASES, WIDTH), F32),
             pltpu.VMEM((32, WIDTH), F32),
-            pltpu.VMEM((CASES, LANES), F32),
+            pltpu.VMEM((CASES, WIDTH), F32),
             pltpu.VMEM((16, LANES), F32),
             dma((6,)),
             dma((4,)),
@@ -604,7 +609,6 @@
         jnp.transpose(modes, (1, 0, 2)),
         coarse,
     )
-    alpha = alpha[:, :1]
     return (alpha * search)[None], (projected - alpha * step)[None]
 
 

time: 70.7 us -> 67 us (0.948)
  Pallas kernels: 67.3 us -> 65.5 us
  other arithmetic: 1.82 us -> 0.73 us
  local copies, waits for them, and re-layouts: 0.83 us -> 0 us
    pallas_call x1, Pallas kernels: 67.3 us -> 65.5 us  [on_device(): pl.pallas_call(functools.partial(kernel, ny, nz, nu), out_shape=(pltpu.VM...]
    broadcast_in_dim x1, other arithmetic: 1.82 us -> 0.73 us  [on_device(): return ((alpha * search)[None], (projected - alpha * step)[None])]
    slice x1 -> x0, local copies, waits for them, and re-layouts: 0.83 us -> none  [on_device(): alpha = alpha[:, :1]]
where the time goes in v4:
time: 67 us; the launch traced here: 66.9 us
  Pallas kernels  65.5 us (98%)
  other arithmetic  0.73 us (1%)
    pallas_call x1, Pallas kernels, on_device(): pl.pallas_call(functools.partial(kernel, ny, nz, nu), out_shape=(pltpu.VM...  65.5 us

profile of v4, /device:TPU:1, one launch (start us, length us, event | category | flops | bytes accessed | tf_op | source)
XLA Modules:
  0.0 66.9 jit_solution(9046578975862834408)
XLA Ops:
  0.6 65.5 %shard_map.77 = (f32[32,1024]{1,0:T(8,128)S(1)}, f32[32,1024]{1,0:T(8,128)S(1)}, f32[32,1024]{1,0:T(8,128)S(1)}, f32[32,1024]{1,0:T(8,128)S(1)}) custom-call(bf16[32,1024]{1,0:T(8,128)(2,1)} %bitcast.10, s32[1,1024]{1,0:T(1,128)} %index_in.1, bf16[1024,1024]{1,0:T(8,128)(2,1)} %bitcast.8, bf16[1024,1024]{1,0:T(8,128)(2,1)} %bitcast.9, ...), custom_call_target="tpu_custom_call" | custom-call | tf_op jit(solution)/shard_map/pallas_call | solution.py:548
  66.2 0.7 %subtract_bitcast_fusion = (f32[1,32,1024]{2,1,0:T(8,128)}, f32[1,32,1024]{2,1,0:T(8,128)}) fusion(f32[32,1024]{1,0:T(8,128)S(1)} %get-tuple-element.8, f32[32,1024]{1,0:T(8,128)S(1)} %get-tuple-element.6, f32[32,1024]{1,0:T(8,128)S(1)} %get-tuple-element.9, f32[32,1024]{1,0:T(8,128)S(1)} %get-tuple-element.7), kind=kLoop, calls=%fused_computation | loop fusion | flops 98304 | bytes 786432 | tf_op jit(solution)/shard_map/broadcast_in_dim | solution.py:612

commit v5 on v4

--- a/solution.py
+++ b/solution.py
@@ -57,8 +57,8 @@
     field, partner, shapes, other_shapes, to_ext,
     coarse_send, coarse_recv, coarse_near, coarse_ext,
     xfirst, xbuf, vpart, vsend, vrecv, vrecv_r,
-    resid, projd, srch, moved, ratio, near_rows,
-    in_sem, out_sem, fsend, frecv, csend, crecv, dsend, drecv, gsend, grecv, psend, precv, nsend, nrecv,
+    resid, projd, srch, moved, near_rows,
+    in_sem, fsend, frecv, csend, crecv, dsend, drecv, gsend, grecv, psend, precv, nsend, nrecv,
 ):
     plane = ny * nu
     r = lax.axis_index("region")
@@ -507,37 +507,31 @@
     srch[...] = srch[...] - rigid_jump(values)
     field[2] = jnp.dot(srch[...].astype(BF16), stiff_s[...], preferred_element_type=F32)
     field_copies.append(exchange(field.at[2], partner.at[2], 2))
-    done = [
-        pltpu.make_async_copy(a, b, out_sem.at[n])
-        for n, (a, b) in enumerate(
-            [(srch, srch_out), (projd, projd_out), (resid, step_out), (ratio, alpha_out)]
-        )
-    ]
-    done[0].start()
-    done[1].start()
+    srch_out[...] = srch[...]
+    projd_out[...] = projd[...]
     send_values(2, ext_product(2))
-    image = jumped(2)
-    values, sums = values_here(2)
-    quotient = pltpu.roll(sums / pltpu.roll(sums, LANES - CASES, 1), 2 * CASES, 1)
-    column = jnp.broadcast_to(quotient, (LANES, LANES)).T[:CASES]
-    ratio[...] = jnp.concatenate([column] * (WIDTH // LANES), axis=1)
-    done[3].start()
-    resid[...] = image - rigid_jump(values)
-    done[2].start()
-    for copy in done:
-        copy.wait()
-
     for copies in field_copies + [shape_copies, near_copies]:
         for copy in copies:
             copy.wait_send()
     wait_bytes(coarse_send.at[pl.ds(0, plane - 1)], csend)
     wait_bytes(xfirst.at[pl.ds(0, nz - 1)], gsend.at[0])
-    for at in range(3):
-        if at:
-            wait_bytes(xbuf.at[at - 1, pl.ds(0, nz - 1)], gsend.at[at])
+    for at in range(2):
+        wait_bytes(xbuf.at[at, pl.ds(0, nz - 1)], gsend.at[at + 1])
+
+    def sent_values(at):
         wait_bytes(vsend.at[at, pl.ds(0, plane - 1)], psend.at[at])
         for n in range(2):
             wait_bytes(vpart.at[at], nsend.at[at, n])
+
+    sent_values(0)
+    sent_values(1)
+    image = jumped(2)
+    values, sums = values_here(2)
+    quotient = pltpu.roll(sums / pltpu.roll(sums, LANES - CASES, 1), 2 * CASES, 1)
+    column = jnp.broadcast_to(quotient, (LANES, LANES)).T[:CASES]
+    alpha_out[...] = jnp.concatenate([column] * (WIDTH // LANES), axis=1)
+    step_out[...] = image - rigid_jump(values)
+    sent_values(2)
 
 
 def on_device(ny, nz, nu, loads, index_blocks, stiffness, dirichlet, modes, coarse):
@@ -581,10 +575,8 @@
             pltpu.VMEM((CASES, WIDTH), F32),
             pltpu.VMEM((CASES, WIDTH), F32),
             pltpu.VMEM((32, WIDTH), F32),
-            pltpu.VMEM((CASES, WIDTH), F32),
             pltpu.VMEM((16, LANES), F32),
             dma((6,)),
-            dma((4,)),
             dma((4, 4)),
             dma((4, 4)),
             dma,

time: 67 us -> 66.4 us (level)
  no operation moved by 1% of the time
where the time goes in v5:
time: 66.4 us; the launch traced here: 66.2 us
  Pallas kernels  64.9 us (98%)
  other arithmetic  0.73 us (1%)
    pallas_call x1, Pallas kernels, on_device(): pl.pallas_call(functools.partial(kernel, ny, nz, nu), out_shape=(pltpu.VM...  64.9 us

profile of v5, /device:TPU:1, one launch (start us, length us, event | category | flops | bytes accessed | tf_op | source)
XLA Modules:
  0.0 66.2 jit_solution(4896677793588334137)
XLA Ops:
  0.6 64.9 %shard_map.77 = (f32[32,1024]{1,0:T(8,128)S(1)}, f32[32,1024]{1,0:T(8,128)S(1)}, f32[32,1024]{1,0:T(8,128)S(1)}, f32[32,1024]{1,0:T(8,128)S(1)}) custom-call(bf16[32,1024]{1,0:T(8,128)(2,1)} %bitcast.10, s32[1,1024]{1,0:T(1,128)} %index_in.1, bf16[1024,1024]{1,0:T(8,128)(2,1)} %bitcast.8, bf16[1024,1024]{1,0:T(8,128)(2,1)} %bitcast.9, ...), custom_call_target="tpu_custom_call" | custom-call | tf_op jit(solution)/shard_map/pallas_call | solution.py:542
  65.5 0.7 %subtract_bitcast_fusion = (f32[1,32,1024]{2,1,0:T(8,128)}, f32[1,32,1024]{2,1,0:T(8,128)}) fusion(f32[32,1024]{1,0:T(8,128)S(1)} %get-tuple-element.8, f32[32,1024]{1,0:T(8,128)S(1)} %get-tuple-element.6, f32[32,1024]{1,0:T(8,128)S(1)} %get-tuple-element.9, f32[32,1024]{1,0:T(8,128)S(1)} %get-tuple-element.7), kind=kLoop, calls=%fused_computation | loop fusion | flops 98304 | bytes 786432 | tf_op jit(solution)/shard_map/broadcast_in_dim | solution.py:604
